TPU v7x, 128 devices: a whole 4x4x4 slice. The times are simulated.
128 devices in a mesh: ty: 8 (over y, x_lo), tx: 16 (over z, x_hi, core).
Axes of the slice: x: 4 (x_hi: 2, x_lo: 2; x = x_hi * 2 + x_lo), y: 4, z: 4, core: 2. Of those that a mesh axis runs over, the one named last changes fastest.
Arguments:
- object_planes: float32 [2, 8192, 8192], P(None, 'ty', 'tx'), may hold values from -6 to 6
- probe: float32 [2, 2, 128, 128], replicated, may hold values from -6 to 6
- positions: int32 [8, 16, 96, 2], P('ty', 'tx'), may hold values from -64 to 8127, as said below
- counts: int32 [8, 16], P('ty', 'tx'), may hold values from 1 to 96, as said below
- amplitudes: float32 [8, 16, 96, 128, 128], P('ty', 'tx'), may hold values from 0.5 to 6
Outputs:
- object_grad: float32 [2, 8192, 8192], P(None, 'ty', 'tx')
- probe_grad: float32 [2, 2, 128, 128], replicated
Inputs may be any that keep to these rules, and one draw needn't show every extreme that they name: `counts`: each tile holds 1 to 96 live positions, some tile exactly 96. `positions`: every slot of tile (i, j), live or not, has its window centre (row + 64, column + 64) inside that tile: rows i * 1024 to (i + 1) * 1024 - 1, columns j * 512 to (j + 1) * 512 - 1.
All inputs are finite; a program needn't handle non-finite values.
Results may differ from a plain program's by a relative error of at most 0.0003.
Values sent between devices are 32-bit elements; how exact they have to be, the bound alone decides.
A program may use at most 192 MiB of HBM per device.

v0:
```python
import math

import jax
import jax.numpy as jnp
from jax import lax
from jax.sharding import PartitionSpec as P

WIN = 128
BLOCK = 16


INTENSITY_FLOOR = 0.25
HIGHEST_PRECISION = lax.Precision.HIGHEST


def extended_2(value, sides, width):
    for axis, dim in sides:
        devices, length = (lax.axis_size(axis), value.shape[dim])
        up = [(i, (i + 1) % devices) for i in range(devices - 1)]
        down = [(j, i) for i, j in up]
        last = lax.slice_in_dim(value, length - width, length, axis=dim)
        first = lax.slice_in_dim(value, 0, width, axis=dim)
        before = lax.ppermute(last, axis, up)
        after = lax.ppermute(first, axis, down)
        value = jnp.concatenate([before, value, after], axis=dim)
    return value


def shifted(value, axis, by):
    devices = lax.axis_size(axis)
    pairs = [(i, i + by) for i in range(devices) if 0 <= i + by < devices]
    return lax.ppermute(value, axis, pairs)


def tables(window):
    index_line = jnp.arange(window, dtype=jnp.int32)
    product = index_line[:, None] * index_line[None, :] % window
    angle = 2.0 * math.pi / window * product.astype(jnp.float32)
    scale = 1.0 / math.sqrt(window)
    cosine_table = jnp.cos(angle) * scale
    sine_table = jnp.sin(angle) * scale
    forward_pair = (
        jnp.concatenate([cosine_table, -sine_table], axis=1),
        jnp.concatenate([sine_table, cosine_table], axis=1),
    )
    inverse_pair = (
        jnp.concatenate([cosine_table, sine_table], axis=1),
        jnp.concatenate([-sine_table, cosine_table], axis=1),
    )
    return (forward_pair, inverse_pair)


def right_apply(real_part, imag_part, matrix_pair):
    first = jnp.einsum("bmjk,kl->bmjl", real_part, matrix_pair[0], precision=HIGHEST_PRECISION)
    return first + jnp.einsum(
        "bmjk,kl->bmjl", imag_part, matrix_pair[1], precision=HIGHEST_PRECISION
    )


def flipped_transform(real_part, imag_part, matrix_pair):
    window = real_part.shape[-1]
    packed = right_apply(real_part, imag_part, matrix_pair)
    turned_re = jnp.swapaxes(packed[..., :window], -1, -2)
    turned_im = jnp.swapaxes(packed[..., window:], -1, -2)
    return right_apply(turned_re, turned_im, matrix_pair)


def position_block(patches, measured, live_mask, probe, forward_pair, inverse_pair):
    window = patches.shape[-1]
    object_re = patches[:, 0][:, None]
    object_im = patches[:, 1][:, None]
    probe_re = probe[:, 0][None]
    probe_im = probe[:, 1][None]
    wave_re = probe_re * object_re - probe_im * object_im
    wave_im = probe_re * object_im + probe_im * object_re
    far_flipped = flipped_transform(wave_re, wave_im, forward_pair)
    far_re = far_flipped[..., :window]
    far_im = far_flipped[..., window:]
    intensity = jnp.sum(far_re * far_re + far_im * far_im, axis=1)
    measured_flipped = jnp.swapaxes(measured, -1, -2)
    weight = (
        1.0 - measured_flipped / jnp.sqrt(jnp.maximum(intensity, INTENSITY_FLOOR))
    ) * live_mask[:, None, None]
    back_packed = flipped_transform(
        weight[:, None] * far_re, weight[:, None] * far_im, inverse_pair
    )
    back_re = back_packed[..., :window]
    back_im = back_packed[..., window:]
    grad_re = jnp.sum(probe_re * back_re + probe_im * back_im, axis=1)
    grad_im = jnp.sum(probe_re * back_im - probe_im * back_re, axis=1)
    term_re = jnp.sum(object_re * back_re + object_im * back_im, axis=0)
    term_im = jnp.sum(object_re * back_im - object_im * back_re, axis=0)
    return (jnp.stack([grad_re, grad_im], axis=1), jnp.stack([term_re, term_im], axis=1))


def extract(planes, row_start, col_start, window):
    anchor = jnp.zeros((), jnp.int32)

    def take_one(row_one, col_one):
        return lax.dynamic_slice(
            planes, (anchor, row_one, col_one), (planes.shape[0], window, window)
        )

    return jax.vmap(take_one)(row_start, col_start)


def deposit(gradient, patch_grads, row_start, col_start):
    anchor = jnp.zeros((), jnp.int32)
    window = patch_grads.shape[2]

    def deposit_one(slot_number, current):
        corner = (anchor, row_start[slot_number], col_start[slot_number])
        present = lax.dynamic_slice(current, corner, (2, window, window))
        return lax.dynamic_update_slice(current, present + patch_grads[slot_number], corner)

    return lax.fori_loop(0, patch_grads.shape[0], deposit_one, gradient)


def run_direct(
    extended, row_start, col_start, measured, live_count, probe, forward_pair, inverse_pair
):
    window = probe.shape[-1]
    block_trips = (live_count + BLOCK - 1) // BLOCK
    offsets = jnp.arange(BLOCK, dtype=jnp.int32)

    def advance(turn_index, state_pair):
        gradient_now, sum_now = state_pair
        start_row = (turn_index * BLOCK).astype(jnp.int32)
        block_rows = lax.dynamic_slice_in_dim(row_start, start_row, BLOCK, 0)
        block_cols = lax.dynamic_slice_in_dim(col_start, start_row, BLOCK, 0)
        block_patches = extract(extended, block_rows, block_cols, window)
        block_measured = lax.dynamic_slice_in_dim(measured, start_row, BLOCK, 0)
        block_live = (start_row + offsets < live_count).astype(jnp.float32)
        block_grads, block_term = position_block(
            block_patches, block_measured, block_live, probe, forward_pair, inverse_pair
        )
        gradient_now = deposit(gradient_now, block_grads, block_rows, block_cols)
        return (gradient_now, sum_now + block_term)

    return lax.fori_loop(
        jnp.int32(0),
        block_trips,
        advance,
        (jnp.zeros_like(extended), jnp.zeros(probe.shape, jnp.float32)),
    )


def shards(object_planes, probe, positions, counts, amplitudes):
    rim_width = WIN // 2
    tile_rows = object_planes.shape[1]
    tile_cols = object_planes.shape[2]
    slot_total = positions.shape[2]
    forward_pair, inverse_pair = tables(WIN)
    extended = extended_2(object_planes, (("ty", 1), ("tx", 2)), rim_width)
    row_base = lax.axis_index("ty") * tile_rows
    col_base = lax.axis_index("tx") * tile_cols
    places = positions[0, 0]
    row_start = places[:, 0] - row_base + rim_width
    col_start = places[:, 1] - col_base + rim_width
    live_count = counts[0, 0]
    measured = amplitudes[0, 0]
    gradient, probe_part = run_direct(
        extended, row_start, col_start, measured, live_count, probe, forward_pair, inverse_pair
    )
    from_right = shifted(gradient[:, :, :rim_width], "tx", -1)
    from_left = shifted(gradient[:, :, tile_cols + rim_width :], "tx", 1)
    gradient = gradient.at[:, :, tile_cols : tile_cols + rim_width].add(from_right)
    gradient = gradient.at[:, :, rim_width : 2 * rim_width].add(from_left)
    gradient = gradient[:, :, rim_width : rim_width + tile_cols]
    from_below = shifted(gradient[:, :rim_width], "ty", -1)
    from_above = shifted(gradient[:, tile_rows + rim_width :], "ty", 1)
    gradient = gradient.at[:, tile_rows : tile_rows + rim_width].add(from_below)
    gradient = gradient.at[:, rim_width : 2 * rim_width].add(from_above)
    object_grad = gradient[:, rim_width : rim_width + tile_rows]
    probe_total = lax.psum(probe_part, ("ty", "tx"))
    probe_grad = probe_total / float(lax.axis_size("ty") * lax.axis_size("tx") * slot_total)
    return (object_grad, probe_grad)


def solution(mesh):
    in_specs = (
        P(None, "ty", "tx"),
        P(),
        P("ty", "tx", None, None),
        P("ty", "tx"),
        P("ty", "tx", None, None, None),
    )
    out_specs = (P(None, "ty", "tx"), P())
    return jax.shard_map(shards, mesh=mesh, in_specs=in_specs, out_specs=out_specs, check_vma=False)
```

profile of v0, /device:TPU:1, one launch (start us, length us, event | category | flops | bytes accessed | tf_op | source)
XLA Modules:
  0.0 1729.5 jit_solution(9018366064395728302)
XLA Ops:
  7.2 5.4 copy.18
  15.3 4.7 collective-permute-start
  20.0 9.0 collective-permute-done.1
  30.1 6.4 concatenate.29
  37.8 6.8 collective-permute-start.2
  47.3 6.6 copy.17
  54.5 5.3 collective-permute-done.3
  59.8 5.2 pad_maximum_fusion.1
  65.0 7.7 copy.22
  75.6 974.9 %while.36 = (s32[]{:T(128)}, f32[2,1152,640]{2,1,0:T(8,128)}, f32[2,2,128,128]{3,2,1,0:T(8,128)S(1)}, s32[]{:T(128)}, s32[96]{0:T(128)S(1)}, /*index=5*/s32[96]{...) while((s32[]{:T(128)}, f32[2,1152,640]{2,1,0:T(8,128)}, ...), condition=%wide.region_8.9_spmd.clone, body=%wide.region_0.8_spmd.clone.sunk | while | flops 12904660992 | bytes 98698808 | solution.py:140
  97.1 47.2 %while.37 = (s32[]{:T(128)}, f32[2,1152,640]{2,1,0:T(8,128)}, s32[16,3]{0,1:T(4,128)S(1)}, f32[16,2,128,128]{3,2,1,0:T(8,128)S(1)}, s32[]{:T(128)}) while((s32[]{:T(128)}, f32[2,1152,640]{2,1,0:T(8,128)}, s32[16,3]{0,1:T(4,128)S(1)}, f32[16,2,128,128]{3,2,1,0:T(8,128)S(1)}, s32[]{:T(128)}) %tuple.118), condition=%wide.while_cond.4, body=%wide.while_body.4.sunk | while | flops 2 | bytes 262269 | solution.py:100
  176.7 158.1 %while.38 = (s32[]{:T(128)}, f32[2,1152,640]{2,1,0:T(8,128)}, s32[16]{0:T(128)S(1)}, s32[16]{0:T(128)S(1)}, f32[16,2,128,128]{3,2,1,0:T(8,128)S(1)}, /*index=5*/s32[]{:T(128)}, s32[]{:T(128)}, s32[]{:T(128)}, s32[]{:T(128)}) while((s32[]{:T(128)}, f32[2,1152,640]{2,1,0:T(8,128)}, s32[16]{0:T(128)S(1)}, s32[16]{0:T(128)S(1)}, ...), condition=%wide.region_5.5_spmd, body=%wide.region_4.4_spmd.sunk | while | flops 32776 | bytes 655569 | solution.py:116
  335.6 47.2 %while.37 = (s32[]{:T(128)}, f32[2,1152,640]{2,1,0:T(8,128)}, s32[16,3]{0,1:T(4,128)S(1)}, f32[16,2,128,128]{3,2,1,0:T(8,128)S(1)}, s32[]{:T(128)}) while((s32[]{:T(128)}, f32[2,1152,640]{2,1,0:T(8,128)}, s32[16,3]{0,1:T(4,128)S(1)}, f32[16,2,128,128]{3,2,1,0:T(8,128)S(1)}, s32[]{:T(128)}) %tuple.118), condition=%wide.while_cond.4, body=%wide.while_body.4.sunk | while | flops 2 | bytes 262269 | solution.py:100
  415.1 158.3 %while.38 = (s32[]{:T(128)}, f32[2,1152,640]{2,1,0:T(8,128)}, s32[16]{0:T(128)S(1)}, s32[16]{0:T(128)S(1)}, f32[16,2,128,128]{3,2,1,0:T(8,128)S(1)}, /*index=5*/s32[]{:T(128)}, s32[]{:T(128)}, s32[]{:T(128)}, s32[]{:T(128)}) while((s32[]{:T(128)}, f32[2,1152,640]{2,1,0:T(8,128)}, s32[16]{0:T(128)S(1)}, s32[16]{0:T(128)S(1)}, ...), condition=%wide.region_5.5_spmd, body=%wide.region_4.4_spmd.sunk | while | flops 32776 | bytes 655569 | solution.py:116
  549.9 3.7 dynamic_update_slice.8
  574.3 47.2 %while.37 = (s32[]{:T(128)}, f32[2,1152,640]{2,1,0:T(8,128)}, s32[16,3]{0,1:T(4,128)S(1)}, f32[16,2,128,128]{3,2,1,0:T(8,128)S(1)}, s32[]{:T(128)}) while((s32[]{:T(128)}, f32[2,1152,640]{2,1,0:T(8,128)}, s32[16,3]{0,1:T(4,128)S(1)}, f32[16,2,128,128]{3,2,1,0:T(8,128)S(1)}, s32[]{:T(128)}) %tuple.118), condition=%wide.while_cond.4, body=%wide.while_body.4.sunk | while | flops 2 | bytes 262269 | solution.py:100
  625.1 3.7 convolution_add_fusion.8
  653.8 158.1 %while.38 = (s32[]{:T(128)}, f32[2,1152,640]{2,1,0:T(8,128)}, s32[16]{0:T(128)S(1)}, s32[16]{0:T(128)S(1)}, f32[16,2,128,128]{3,2,1,0:T(8,128)S(1)}, /*index=5*/s32[]{:T(128)}, s32[]{:T(128)}, s32[]{:T(128)}, s32[]{:T(128)}) while((s32[]{:T(128)}, f32[2,1152,640]{2,1,0:T(8,128)}, s32[16]{0:T(128)S(1)}, s32[16]{0:T(128)S(1)}, ...), condition=%wide.region_5.5_spmd, body=%wide.region_4.4_spmd.sunk | while | flops 32776 | bytes 655569 | solution.py:116
  670.0 3.8 dynamic_update_slice.8
  699.7 3.8 dynamic_update_slice.8
  812.8 47.2 %while.37 = (s32[]{:T(128)}, f32[2,1152,640]{2,1,0:T(8,128)}, s32[16,3]{0,1:T(4,128)S(1)}, f32[16,2,128,128]{3,2,1,0:T(8,128)S(1)}, s32[]{:T(128)}) while((s32[]{:T(128)}, f32[2,1152,640]{2,1,0:T(8,128)}, s32[16,3]{0,1:T(4,128)S(1)}, f32[16,2,128,128]{3,2,1,0:T(8,128)S(1)}, s32[]{:T(128)}) %tuple.118), condition=%wide.while_cond.4, body=%wide.while_body.4.sunk | while | flops 2 | bytes 262269 | solution.py:100
  863.6 3.7 convolution_add_fusion.8
  892.4 158.2 %while.38 = (s32[]{:T(128)}, f32[2,1152,640]{2,1,0:T(8,128)}, s32[16]{0:T(128)S(1)}, s32[16]{0:T(128)S(1)}, f32[16,2,128,128]{3,2,1,0:T(8,128)S(1)}, /*index=5*/s32[]{:T(128)}, s32[]{:T(128)}, s32[]{:T(128)}, s32[]{:T(128)}) while((s32[]{:T(128)}, f32[2,1152,640]{2,1,0:T(8,128)}, s32[16]{0:T(128)S(1)}, s32[16]{0:T(128)S(1)}, ...), condition=%wide.region_5.5_spmd, body=%wide.region_4.4_spmd.sunk | while | flops 32776 | bytes 655569 | solution.py:116
  1050.6 7.8 copy.25
  1061.6 5.1 collective-permute-start.5
  1066.8 11.3 collective-permute-done.4
  1084.8 602.4 %all-reduce.2.cloned.1.call-done = f32[2,2,128,128]{3,2,1,0:T(8,128)} async-done(((f32[2,2,128,128]{3,2,1,0:T(8,128)}), f32[2,2,128,128]{3,2,1,0:T(8,128)}) %all-reduce.2.cloned.1.call-update) | async-done | bytes 262160 | tf_op jit(solution)/shard_map/psum | solution.py:175
  1688.8 4.8 slice.230
  1700.2 6.2 collective-permute-done.7
  1707.6 3.9 scatter-add.19
  1711.5 5.4 slice.235
  1716.9 5.4 copy.27
  (557 shorter events, 718.9 us)
Async XLA Ops:
  7.2 1680.0 %all-reduce.2.cloned.1.call-start = ((), (), s32[]{:S(2)}) async-start(), calls=%async_computation | async-start | bytes 524288 | tf_op jit(solution)/shard_map/psum | solution.py:175
  14.0 15.1 collective-permute-start.1
  15.3 32.0 %copy-start.1 = (f32[2,2,128,128]{3,2,1,0:T(8,128)S(1)}, f32[2,2,128,128]{3,2,1,0:T(8,128)}, u32[]{:S(2)}) copy-start(f32[2,2,128,128]{3,2,1,0:T(8,128)} %param.18) | copy-start | bytes 786436
  15.3 14.8 collective-permute-start
  37.8 16.7 collective-permute-start.2
  44.6 15.1 collective-permute-start.3
  47.3 7.2 copy-start.2
  1050.6 7.8 copy-start
  1059.7 18.4 %collective-permute-start.4 = (f32[2,1152,64]{1,2,0:T(8,128)S(1)}, f32[2,1152,64]{1,2,0:T(8,128)S(1)}, u32[]{:S(2)}, u32[]{:S(2)}) collective-permute-start(f32[2,1152,64]{1,2,0:T(8,128)S(1)} %get-tuple-element.363), channel_id=1, source_target_pairs={{1,0},{2,1},{3,2},{4,3},{5,4},{6,5},{7,6},{8,7},{9,8},{10,9},{11,1... | collective-permute-start | bytes 1769480 | tf_op jit(solution)/shard_map/ppermute | solution.py:32
  1061.6 18.5 %collective-permute-start.5 = (f32[2,1152,64]{1,2,0:T(8,128)S(1)}, f32[2,1152,64]{1,2,0:T(8,128)S(1)}, u32[]{:S(2)}, u32[]{:S(2)}) collective-permute-start(f32[2,1152,64]{1,2,0:T(8,128)S(1)} %get-tuple-element.362), channel_id=1, source_target_pairs={{0,1},{1,2},{2,3},{3,4},{4,5},{5,6},{6,7},{7,8},{8,9},{9,10},{10,1... | collective-permute-start | bytes 1769480 | tf_op jit(solution)/shard_map/ppermute | solution.py:32
  1083.5 612.8 %collective-permute-start.6 = (f32[2,64,512]{1,2,0:T(8,128)S(1)}, f32[2,64,512]{1,2,0:T(8,128)S(1)}, u32[]{:S(2)}, u32[]{:S(2)}) collective-permute-start(f32[2,64,512]{1,2,0:T(8,128)S(1)} %get-tuple-element.361), channel_id=1, source_target_pairs={{16,0},{32,16},{48,32},{64,48},{80,64},{96,80},{112,96},{17,1},{33... | collective-permute-start | bytes 786440 | tf_op jit(solution)/shard_map/ppermute | solution.py:32
  1693.7 12.7 collective-permute-start.7
Sparse Core Ops, SparseCore 0:
  1066.9 620.1 all-reduce.1
where the time goes:
time: 1760 us; the launch traced here: 1730 us
  waiting for transfers between devices  635 us (36%)
  local copies, waits for them, and re-layouts  571 us (32%)
  loops' own time  267 us (15%)
  matrix products  116 us (7%)
  other arithmetic  99 us (6%)
  starting transfers between devices  25.8 us (1%)
    psum x1, waiting for transfers between devices, shards(): probe_total = lax.psum(probe_part, ('ty', 'tx'))  602 us
    another operation x4, loops' own time, deposit(): return lax.fori_loop(0, patch_grads.shape[0], deposit_one, gradient)  245 us
    dynamic_update_slice x64, local copies, waits for them, and re-layouts, deposit_one(): lax.dynamic_update_slice(current, present + patch_grads[slot_number], cor...  235 us
    gather x192, local copies, waits for them, and re-layouts  188 us
    dynamic_slice x128, local copies, waits for them, and re-layouts, deposit_one(): corner = (anchor, row_start[slot_number], col_start[slot_number])  83.4 us
    add x64, other arithmetic, deposit_one(): present + patch_grads[slot_number]  69.2 us
    dot_general x16, matrix products, right_apply(): jnp.einsum('bmjk,kl->bmjl', imag_part, matrix_pair[1], precision=HIGHEST_...  58.3 us
    dot_general x16, matrix products, right_apply(): jnp.einsum('bmjk,kl->bmjl', real_part, matrix_pair[0], precision=HIGHEST_...  57.3 us
  transfers between devices with their start and end apart: 9, of which 6 were waited for; matrix products, arithmetic and copies ran while one was open for 1% of the time, Pallas kernels for 0%

commit v1 on v0

v1 whole, which is shorter than its diff:
```python
import functools
import math

import jax
import jax.numpy as jnp
import numpy as np
from jax import lax
from jax.experimental import pallas as pl
from jax.experimental.pallas import tpu as pltpu
from jax.sharding import PartitionSpec as P

WIN = 128
RIM = WIN // 2
FLOOR = 0.25
AHEAD = 4


def matrices():
    index = np.arange(WIN)
    angle = 2.0 * math.pi / WIN * ((index[:, None] * index[None, :]) % WIN)
    cosine = np.cos(angle) / math.sqrt(WIN)
    sine = np.sin(angle) / math.sqrt(WIN)
    right = np.block([[cosine, -sine], [sine, cosine]])
    both = np.stack([right, right.T]).astype(np.float32)
    high = both.astype(jnp.bfloat16)
    low = (both - high.astype(np.float32)).astype(jnp.bfloat16)
    return np.stack([high, low], axis=1)


def split(value):
    high = value.astype(jnp.bfloat16)
    low = (value - high.astype(jnp.float32)).astype(jnp.bfloat16)
    return high, low


def dot(a, b):
    return lax.dot_general(a, b, (((1,), (0,)), ((), ())), preferred_element_type=jnp.float32)


def right_product(value, high_w, low_w):
    high, low = split(value)
    return dot(high, high_w) + dot(low, high_w) + dot(high, low_w)


def left_product(value, high_w, low_w):
    high, low = split(value)
    return dot(high_w, high) + dot(high_w, low) + dot(low_w, high)


def blocks(value):
    n = WIN
    return value[:n, :n], value[:n, n:], value[n:, :n], value[n:, n:]


def assemble(a, b, c, d):
    top = jnp.concatenate([a, b], axis=1)
    bottom = jnp.concatenate([c, d], axis=1)
    return jnp.concatenate([top, bottom], axis=0)


def slot_gradient(window_re, window_im, probe_ref, measured, live, w_ref):
    p0r, p0i = probe_ref[0, 0], probe_ref[0, 1]
    p1r, p1i = probe_ref[1, 0], probe_ref[1, 1]
    wave = assemble(
        p0r * window_re - p0i * window_im,
        p0r * window_im + p0i * window_re,
        p1r * window_re - p1i * window_im,
        p1r * window_im + p1i * window_re,
    )
    half = right_product(wave, w_ref[0, 0], w_ref[0, 1])
    m0r, m0i, m1r, m1i = blocks(half)
    far = left_product(assemble(m0r, m1r, m0i, m1i), w_ref[1, 0], w_ref[1, 1])
    f0r, f1r, f0i, f1i = blocks(far)
    intensity = f0r * f0r + f0i * f0i + (f1r * f1r + f1i * f1i)
    weight = live - (live * measured) * lax.rsqrt(jnp.maximum(intensity, FLOOR))
    half = left_product(
        assemble(weight * f0r, weight * f1r, weight * f0i, weight * f1i), w_ref[0, 0], w_ref[0, 1]
    )
    m0r, m1r, m0i, m1i = blocks(half)
    back = right_product(assemble(m0r, m0i, m1r, m1i), w_ref[1, 0], w_ref[1, 1])
    b0r, b0i, b1r, b1i = blocks(back)
    grad_re = p0r * b0r + p0i * b0i + (p1r * b1r + p1i * b1i)
    grad_im = p0r * b0i - p0i * b0r + (p1r * b1i - p1i * b1r)
    terms = (
        window_re * b0r + window_im * b0i,
        window_re * b0i - window_im * b0r,
        window_re * b1r + window_im * b1i,
        window_re * b1i - window_im * b1r,
    )
    return grad_re, grad_im, terms


def body(
    count_ref, place_ref, probe_ref, w_ref, tile_ref, left_ref, right_ref, top_ref, bottom_ref, measured_ref,
    grad_tile, grad_left, grad_right, grad_top, grad_bottom, probe_out,
    obj, grad, held, in_sems, held_sems,
):
    rows = tile_ref.shape[1]
    cols = tile_ref.shape[2]
    tiles = cols // WIN
    count = count_ref[0, 0]
    lane = lax.broadcasted_iota(jnp.int32, (WIN, WIN), 1)

    def fetch(slot):
        return pltpu.make_async_copy(
            measured_ref.at[slot], held.at[lax.rem(slot, AHEAD)], held_sems.at[lax.rem(slot, AHEAD)]
        )

    for ahead in range(AHEAD):
        @pl.when(ahead < count)
        def _(ahead=ahead):
            fetch(jnp.int32(ahead)).start()

    loads = []
    for q in range(tiles):
        span = pl.ds(q * WIN, WIN)
        loads.append((tile_ref.at[:, :, span], obj.at[:, q + 1, pl.ds(RIM, rows), :]))
        loads.append((top_ref.at[:, :, span], obj.at[:, q + 1, pl.ds(0, RIM), :]))
        loads.append((bottom_ref.at[:, :, span], obj.at[:, q + 1, pl.ds(RIM + rows, RIM), :]))
    loads.append((left_ref, obj.at[:, 0]))
    loads.append((right_ref, obj.at[:, tiles + 1]))
    loads = [pltpu.make_async_copy(a, b, in_sems.at[i]) for i, (a, b) in enumerate(loads)]
    for copy in loads:
        copy.start()
    grad[...] = jnp.zeros_like(grad)
    probe_out[...] = jnp.zeros_like(probe_out)
    for copy in loads:
        copy.wait()

    @pl.loop(0, count)
    def _(slot):
        row = place_ref[slot, 0]
        col = place_ref[slot, 1]
        q = col // WIN
        shift = lax.rem(col, WIN)
        here = pl.ds(row, WIN)
        keep = lane < WIN - shift
        window = []
        for plane in range(2):
            first = pltpu.roll(obj[plane, q, here, :], WIN - shift, 1)
            second = pltpu.roll(obj[plane, q + 1, here, :], WIN - shift, 1)
            window.append(jnp.where(keep, first, second))
        fetch(slot).wait()
        measured = held[lax.rem(slot, AHEAD)]
        grad_re, grad_im, terms = slot_gradient(window[0], window[1], probe_ref, measured, 1.0, w_ref)

        @pl.when(slot + AHEAD < count)
        def _():
            fetch(slot + AHEAD).start()

        after = lane >= shift
        for plane, value in enumerate((grad_re, grad_im)):
            turned = pltpu.roll(value, shift, 1)
            grad[plane, q, here, :] += jnp.where(after, turned, 0.0)
            grad[plane, q + 1, here, :] += jnp.where(after, 0.0, turned)
        for i, term in enumerate(terms):
            probe_out[i // 2, i % 2] += term

    stores = []
    for q in range(tiles):
        span = pl.ds(q * WIN, WIN)
        stores.append((grad.at[:, q + 1, pl.ds(RIM, rows), :], grad_tile.at[:, :, span]))
        stores.append((grad.at[:, q + 1, pl.ds(0, RIM), :], grad_top.at[:, :, span]))
        stores.append((grad.at[:, q + 1, pl.ds(RIM + rows, RIM), :], grad_bottom.at[:, :, span]))
    stores.append((grad.at[:, 0], grad_left))
    stores.append((grad.at[:, tiles + 1], grad_right))
    stores = [pltpu.make_async_copy(a, b, in_sems.at[i]) for i, (a, b) in enumerate(stores)]
    for copy in stores:
        copy.start()
    for copy in stores:
        copy.wait()


def tile_gradient(count, places, probe, tile, left, right, top, bottom, measured):
    planes, rows, cols = tile.shape
    tiles = cols // WIN
    f32 = jnp.float32
    smem = pl.BlockSpec(memory_space=pltpu.SMEM)
    vmem = pl.BlockSpec(memory_space=pltpu.VMEM)
    hbm = pl.BlockSpec(memory_space=pl.ANY)
    extent = (planes, tiles + 2, rows + WIN, WIN)
    copies = 3 * tiles + 2
    return pl.pallas_call(
        body,
        out_shape=(
            jax.ShapeDtypeStruct(tile.shape, f32),
            jax.ShapeDtypeStruct(left.shape, f32),
            jax.ShapeDtypeStruct(right.shape, f32),
            jax.ShapeDtypeStruct(top.shape, f32),
            jax.ShapeDtypeStruct(bottom.shape, f32),
            jax.ShapeDtypeStruct(probe.shape, f32),
        ),
        in_specs=[smem, smem, vmem, vmem, hbm, hbm, hbm, hbm, hbm, hbm],
        out_specs=(hbm, hbm, hbm, hbm, hbm, vmem),
        scratch_shapes=[
            pltpu.VMEM(extent, f32),
            pltpu.VMEM(extent, f32),
            pltpu.VMEM((AHEAD, WIN, WIN), f32),
            pltpu.SemaphoreType.DMA((copies,)),
            pltpu.SemaphoreType.DMA((AHEAD,)),
        ],
        compiler_params=pltpu.CompilerParams(vmem_limit_bytes=48 * 1024 * 1024),
        name="tile_gradient",
    )(count, places, probe, jnp.asarray(matrices()), tile, left, right, top, bottom, measured)


def shifted(value, axis, by):
    devices = lax.axis_size(axis)
    pairs = [(i, i + by) for i in range(devices) if 0 <= i + by < devices]
    return lax.ppermute(value, axis, pairs)


def shards(object_planes, probe, positions, counts, amplitudes):
    planes, rows, cols = object_planes.shape
    top = shifted(object_planes[:, rows - RIM :], "ty", 1)
    bottom = shifted(object_planes[:, :RIM], "ty", -1)
    tall_last = jnp.concatenate(
        [top[:, :, cols - RIM :], object_planes[:, :, cols - RIM :], bottom[:, :, cols - RIM :]], axis=1
    )
    tall_first = jnp.concatenate([top[:, :, :RIM], object_planes[:, :, :RIM], bottom[:, :, :RIM]], axis=1)
    left = jnp.pad(shifted(tall_last, "tx", 1), ((0, 0), (0, 0), (RIM, 0)))
    right = jnp.pad(shifted(tall_first, "tx", -1), ((0, 0), (0, 0), (0, RIM)))
    base = jnp.stack([lax.axis_index("ty") * rows - RIM, lax.axis_index("tx") * cols - WIN]).astype(jnp.int32)
    places = positions[0, 0] - base
    g_tile, g_left, g_right, g_top, g_bottom, probe_part = tile_gradient(
        counts, places, probe, object_planes, left, right, top, bottom, amplitudes[0, 0]
    )
    from_right = shifted(g_left[:, :, RIM:], "tx", -1)
    from_left = shifted(g_right[:, :, :RIM], "tx", 1)
    g_top = g_top.at[:, :, cols - RIM :].add(from_right[:, :RIM]).at[:, :, :RIM].add(from_left[:, :RIM])
    g_bottom = g_bottom.at[:, :, cols - RIM :].add(from_right[:, RIM + rows :])
    g_bottom = g_bottom.at[:, :, :RIM].add(from_left[:, RIM + rows :])
    from_below = shifted(g_top, "ty", -1)
    from_above = shifted(g_bottom, "ty", 1)
    out = g_tile.at[:, :, cols - RIM :].add(from_right[:, RIM : RIM + rows])
    out = out.at[:, :, :RIM].add(from_left[:, RIM : RIM + rows])
    out = out.at[:, rows - RIM :].add(from_below).at[:, :RIM].add(from_above)
    total = lax.psum(probe_part, ("ty", "tx"))
    slots = lax.axis_size("ty") * lax.axis_size("tx") * positions.shape[2]
    return out, total / float(slots)


def solution(mesh):
    in_specs = (
        P(None, "ty", "tx"),
        P(),
        P("ty", "tx", None, None),
        P("ty", "tx"),
        P("ty", "tx", None, None, None),
    )
    out_specs = (P(None, "ty", "tx"), P())
    return jax.shard_map(shards, mesh=mesh, in_specs=in_specs, out_specs=out_specs, check_vma=False)
```

time: 1760 us -> 386 us (0.22); the launches traced: 1730 us -> 384 us
  local copies, waits for them, and re-layouts: 571 us -> 30.8 us
  waiting for transfers between devices: 635 us -> 266 us
  loops' own time: 267 us -> 0 us
  matrix products: 116 us -> 0 us
  other arithmetic: 99 us -> 8.39 us
  Pallas kernels: 0 us -> 27.3 us
    psum x1, waiting for transfers between devices: 602 us -> 254 us  [shards(): total = lax.psum(probe_part, ('ty', 'tx'))]
    another operation x9 -> x0, loops' own time: 267 us -> none  [the longest x4 245 us: deposit(): return lax.fori_loop(0, patch_grads.shape[0], deposit_one, gradient)]
    dynamic_update_slice x64 -> x0, local copies, waits for them, and re-layouts: 235 us -> none  [deposit_one(): lax.dynamic_update_slice(current, present + patch_grads[slot_number], cor...]
    gather x192 -> x0, local copies, waits for them, and re-layouts: 188 us -> none
    dot_general x32 -> x0, matrix products: 116 us -> none  [the longest x16 58.3 us: right_apply(): jnp.einsum('bmjk,kl->bmjl', imag_part, matrix_pair[1], precision=HIGHEST_...]
    dynamic_slice x128 -> x0, local copies, waits for them, and re-layouts: 83.4 us -> none  [deposit_one(): corner = (anchor, row_start[slot_number], col_start[slot_number])]
    add x71 -> x6, other arithmetic: 71.8 us -> 3.1 us  [the longest x1 1.57 us: shards(): out = g_tile.at[:, :, cols - RIM:].add(from_right[:, RIM:RIM + rows])]
    pallas_call x0 -> x1, Pallas kernels: none -> 27.3 us  [tile_gradient(): pl.pallas_call(body, out_shape=(jax.ShapeDtypeStruct(tile.shape, f32), ja...]
  transfers between devices with their start and end apart: 9 -> 9, of which waited for: 6 -> 4; matrix products, arithmetic and copies ran while one was open for 1% -> 8% of each run, Pallas kernels for 0% -> 0%
where the time goes in v1:
time: 386 us; the launch traced here: 384 us
  waiting for transfers between devices  266 us (69%)
  starting transfers between devices  36.1 us (9%)
  local copies, waits for them, and re-layouts  30.8 us (8%)
  Pallas kernels  27.3 us (7%)
  between operations  15.1 us (4%)
  other arithmetic  8.39 us (2%)
    psum x1, waiting for transfers between devices, shards(): total = lax.psum(probe_part, ('ty', 'tx'))  254 us
    ppermute x8, starting transfers between devices, shifted(): return lax.ppermute(value, axis, pairs)  36 us
    pallas_call x1, Pallas kernels, tile_gradient(): pl.pallas_call(body, out_shape=(jax.ShapeDtypeStruct(tile.shape, f32), ja...  27.3 us
    ppermute x8, waiting for transfers between devices, shifted(): return lax.ppermute(value, axis, pairs)  12.1 us
  transfers between devices with their start and end apart: 9, of which 4 were waited for; matrix products, arithmetic and copies ran while one was open for 8% of the time, Pallas kernels for 0%

profile of v1, /device:TPU:1, one launch (start us, length us, event | category | flops | bytes accessed | tf_op | source)
XLA Modules:
  0.0 383.8 jit_solution(15584360507665733924)
XLA Ops:
  7.2 1.8 fusion.3
  9.0 3.9 %collective-permute-start = (f32[2,64,512]{2,1,0:T(8,128)}, f32[2,64,512]{2,1,0:T(8,128)S(1)}, u32[]{:S(2)}, u32[]{:S(2)}) collective-permute-start(f32[2,64,512]{2,1,0:T(8,128)} %get-tuple-element.113), channel_id=1, source_target_pairs={{0,16},{16,32},{32,48},{48,64},{64,80},{80,96},{96,112},{1,17},{17... | collective-permute-start | bytes 786440 | tf_op jit(solution)/shard_map/ppermute | solution.py:210
  12.9 1.3 collective-permute-start.1
  14.2 1.9 fusion.2
  16.2 1.1 copy.27
  17.6 0.6 collective-permute-done.top_ref
  18.4 7.3 %collective-permute-done.1.bottom_ref = f32[2,64,512]{2,1,0:T(8,128)S(1)} collective-permute-done((f32[2,64,512]{2,1,0:T(8,128)S(1)}, f32[2,64,512]{2,1,0:T(8,128)S(1)}, u32[]{:S(2)}, u32[]{:S(2)}) %collective-permute-start.1) | collective-permute-done | bytes 262176 | tf_op jit(solution)/shard_map/ppermute | solution.py:210
  25.9 1.4 concatenate.23
  27.3 3.5 collective-permute-start.3
  30.9 1.0 concatenate.22
  31.9 4.5 %collective-permute-start.2 = (f32[2,1152,64]{1,2,0:T(8,128)}, f32[2,1152,64]{1,2,0:T(8,128)}, u32[]{:S(2)}, u32[]{:S(2)}) collective-permute-start(f32[2,1152,64]{1,2,0:T(8,128)} %concatenate.22), channel_id=1, source_target_pairs={{0,1},{1,2},{2,3},{3,4},{4,5},{5,6},{6,7},{7,8},{8,9},{9,10},{10,1... | collective-permute-start | bytes 1769480 | tf_op jit(solution)/shard_map/ppermute | solution.py:210
  37.4 4.1 %collective-permute-done.3 = f32[2,1152,64]{1,2,0:T(8,128)} collective-permute-done((f32[2,1152,64]{1,2,0:T(8,128)S(1)}, f32[2,1152,64]{1,2,0:T(8,128)}, u32[]{:S(2)}, u32[]{:S(2)}) %collective-permute-start.3) | collective-permute-done | bytes 589856 | tf_op jit(solution)/shard_map/ppermute | solution.py:210
  41.5 1.4 copy.17
  43.0 1.1 pad.25.right_ref
  44.1 1.4 copy.13
  45.9 27.3 %tile_gradient.1 = (f32[2,1024,512]{2,1,0:T(8,128)}, f32[2,1152,128]{2,1,0:T(8,128)S(1)}, f32[2,1152,128]{2,1,0:T(8,128)S(1)}, f32[2,64,512]{2,1,0:T(8,128)S(1)}...) custom-call(s32[1,1]{1,0:T(1,128)S(6)} %copy.43.count_ref, s32[96,2]{1,0:T(8,128)S(1)} %bitcast_subtract_fusion.place_ref, ...), custom_call_target="tpu_custom_call" | custom-call | tf_op jit(solution)/shard_map/tile_gradient/pallas_call | solution.py:183
  73.6 1.2 copy.18
  74.8 1.9 collective-permute-start.4
  76.7 1.2 copy.20
  77.9 16.3 %collective-permute-start.5 = (f32[2,1152,64]{1,2,0:T(8,128)}, f32[2,1152,64]{1,2,0:T(8,128)S(1)}, u32[]{:S(2)}, u32[]{:S(2)}) collective-permute-start(f32[2,1152,64]{1,2,0:T(8,128)} %copy.20), channel_id=1, source_target_pairs={{0,1},{1,2},{2,3},{3,4},{4,5},{5,6},{6,7},{7,8},{8,9},{9,10},{10,1... | collective-permute-start | bytes 1769480 | tf_op jit(solution)/shard_map/ppermute | solution.py:210
  94.2 254.2 %all-reduce.4.cloned.1.call-done = f32[2,2,128,128]{3,2,1,0:T(8,128)} async-done(((f32[2,2,128,128]{3,2,1,0:T(8,128)}), f32[2,2,128,128]{3,2,1,0:T(8,128)}) %all-reduce.4.cloned.1.call-update) | async-done | bytes 262160 | tf_op jit(solution)/shard_map/psum | solution.py:238
  348.4 1.7 broadcast_multiply_fusion
  350.5 0.6 scatter-add.35
  351.7 3.3 collective-permute-start.7
  355.1 0.6 scatter-add.30
  356.3 1.3 collective-permute-start.6
  358.2 1.6 slice_add_fusion.1
  359.7 6.0 %scatter-add.26 = f32[2,1024,512]{2,1,0:T(8,128)} dynamic-update-slice(f32[2,1024,512]{2,1,0:T(8,128)} %get-tuple-element.104, f32[2,1024,64]{2,1,0:T(8,128)S(1)} %slice_add_fusion.1, s32[]{:T(128)} %constant.211.clone.1, s32[]{:T(128)} %constant.211.clone.1, s32[]{:T(128)} %constant.212.clone.1) | dynamic-update-slice | bytes 1048580 | tf_op jit(solution)/shard_map/scatter-add | solution.py:235
  366.2 1.3 slice_add_fusion
  367.6 5.9 %scatter-add.29 = f32[2,1024,512]{2,1,0:T(8,128)} dynamic-update-slice(f32[2,1024,512]{2,1,0:T(8,128)} %scatter-add.26, f32[2,1024,64]{2,1,0:T(8,128)S(1)} %slice_add_fusion, s32[]{:T(128)} %constant.211.clone.1, s32[]{:T(128)} %constant.211.clone.1, s32[]{:T(128)} %constant.211.clone.1) | dynamic-update-slice | bytes 1048580 | tf_op jit(solution)/shard_map/scatter-add | solution.py:236
  373.4 1.8 fusion.1
  375.2 1.8 fusion
  (41 shorter events, 4.5 us)
Async XLA Ops:
  7.2 341.2 %all-reduce.4.cloned.1.call-start = ((), (), s32[]{:S(2)}) async-start(), calls=%async_computation | async-start | bytes 524288 | tf_op jit(solution)/shard_map/psum | solution.py:238
  9.0 9.2 %collective-permute-start = (f32[2,64,512]{2,1,0:T(8,128)}, f32[2,64,512]{2,1,0:T(8,128)S(1)}, u32[]{:S(2)}, u32[]{:S(2)}) collective-permute-start(f32[2,64,512]{2,1,0:T(8,128)} %get-tuple-element.113), channel_id=1, source_target_pairs={{0,16},{16,32},{32,48},{48,64},{64,80},{80,96},{96,112},{1,17},{17... | collective-permute-start | bytes 786440 | tf_op jit(solution)/shard_map/ppermute | solution.py:210
  12.9 12.8 %collective-permute-start.1 = (f32[2,64,512]{2,1,0:T(8,128)S(1)}, f32[2,64,512]{2,1,0:T(8,128)S(1)}, u32[]{:S(2)}, u32[]{:S(2)}) collective-permute-start(f32[2,64,512]{2,1,0:T(8,128)S(1)} %get-tuple-element.112), channel_id=1, source_target_pairs={{16,0},{32,16},{48,32},{64,48},{80,64},{96,80},{112,96},{17,1},{33... | collective-permute-start | bytes 786440 | tf_op jit(solution)/shard_map/ppermute | solution.py:210
  16.1 20.4 %copy-start.2 = (s32[1,1,96,2]{2,3,1,0:T(2,128)S(1)}, s32[1,1,96,2]{2,3,1,0:T(2,128)}, u32[]{:S(2)}) copy-start(s32[1,1,96,2]{2,3,1,0:T(2,128)} %param.24) | copy-start | bytes 2308
  27.3 14.3 %collective-permute-start.3 = (f32[2,1152,64]{1,2,0:T(8,128)S(1)}, f32[2,1152,64]{1,2,0:T(8,128)}, u32[]{:S(2)}, u32[]{:S(2)}) collective-permute-start(f32[2,1152,64]{1,2,0:T(8,128)S(1)} %concatenate.23), channel_id=1, source_target_pairs={{1,0},{2,1},{3,2},{4,3},{5,4},{6,5},{7,6},{8,7},{9,8},{10,9},{11,1... | collective-permute-start | bytes 1769480 | tf_op jit(solution)/shard_map/ppermute | solution.py:210
  31.9 12.2 %collective-permute-start.2 = (f32[2,1152,64]{1,2,0:T(8,128)}, f32[2,1152,64]{1,2,0:T(8,128)}, u32[]{:S(2)}, u32[]{:S(2)}) collective-permute-start(f32[2,1152,64]{1,2,0:T(8,128)} %concatenate.22), channel_id=1, source_target_pairs={{0,1},{1,2},{2,3},{3,4},{4,5},{5,6},{6,7},{7,8},{8,9},{9,10},{10,1... | collective-permute-start | bytes 1769480 | tf_op jit(solution)/shard_map/ppermute | solution.py:210
  36.6 9.3 %copy-start = (bf16[2,2,256,256]{3,2,1,0:T(8,128)(2,1)S(1)}, bf16[2,2,256,256]{3,2,1,0:T(8,128)(2,1)}, u32[]{:S(2)}) copy-start(bf16[2,2,256,256]{3,2,1,0:T(8,128)(2,1)} %constant.215.clone.w_ref) | copy-start | bytes 1572868
  36.6 9.3 %copy-start.1 = (f32[2,2,128,128]{3,2,1,0:T(8,128)S(1)}, f32[2,2,128,128]{3,2,1,0:T(8,128)}, u32[]{:S(2)}) copy-start(f32[2,2,128,128]{3,2,1,0:T(8,128)} %probe_ref.1) | copy-start | bytes 786436
  74.8 275.3 %collective-permute-start.4 = (f32[2,1152,64]{1,2,0:T(8,128)}, f32[2,1152,64]{1,2,0:T(8,128)S(1)}, u32[]{:S(2)}, u32[]{:S(2)}) collective-permute-start(f32[2,1152,64]{1,2,0:T(8,128)} %copy.18), channel_id=1, source_target_pairs={{1,0},{2,1},{3,2},{4,3},{5,4},{6,5},{7,6},{8,7},{9,8},{10,9},{11,1... | collective-permute-start | bytes 1769480 | tf_op jit(solution)/shard_map/ppermute | solution.py:210
  77.9 272.4 %collective-permute-start.5 = (f32[2,1152,64]{1,2,0:T(8,128)}, f32[2,1152,64]{1,2,0:T(8,128)S(1)}, u32[]{:S(2)}, u32[]{:S(2)}) collective-permute-start(f32[2,1152,64]{1,2,0:T(8,128)} %copy.20), channel_id=1, source_target_pairs={{0,1},{1,2},{2,3},{3,4},{4,5},{5,6},{6,7},{7,8},{8,9},{9,10},{10,1... | collective-permute-start | bytes 1769480 | tf_op jit(solution)/shard_map/ppermute | solution.py:210
  351.7 23.6 %collective-permute-start.7 = (f32[2,64,512]{2,1,0:T(8,128)S(1)}, f32[2,64,512]{2,1,0:T(8,128)}, u32[]{:S(2)}, u32[]{:S(2)}) collective-permute-start(f32[2,64,512]{2,1,0:T(8,128)S(1)} %scatter-add.36), channel_id=1, source_target_pairs={{0,16},{16,32},{32,48},{48,64},{64,80},{80,96},{96,112},{1,17},{17... | collective-permute-start | bytes 786440 | tf_op jit(solution)/shard_map/ppermute | solution.py:210
  356.3 17.1 %collective-permute-start.6 = (f32[2,64,512]{2,1,0:T(8,128)S(1)}, f32[2,64,512]{2,1,0:T(8,128)}, u32[]{:S(2)}, u32[]{:S(2)}) collective-permute-start(f32[2,64,512]{2,1,0:T(8,128)S(1)} %scatter-add.31), channel_id=1, source_target_pairs={{16,0},{32,16},{48,32},{64,48},{80,64},{96,80},{112,96},{17,1},{33... | collective-permute-start | bytes 786440 | tf_op jit(solution)/shard_map/ppermute | solution.py:210
Sparse Core Ops, SparseCore 0:
  76.8 271.5 all-reduce.3

commit v2 on v1

v2 whole, which is shorter than its diff:
```python
import math

import jax
import jax.numpy as jnp
import numpy as np
from jax import lax
from jax.experimental import pallas as pl
from jax.experimental.pallas import tpu as pltpu
from jax.sharding import PartitionSpec as P

WIN = 128
RIM = WIN // 2
FLOOR = 0.25
AHEAD = 16
MESH = pl.DeviceIdType.MESH
SLOTS_ALL = 8 * 16 * 96
U = 8
SLOTS = 96


def matrices():
    index = np.arange(WIN)
    angle = 2.0 * math.pi / WIN * ((index[:, None] * index[None, :]) % WIN)
    cosine = np.cos(angle) / math.sqrt(WIN)
    sine = np.sin(angle) / math.sqrt(WIN)
    right = np.block([[cosine, -sine], [sine, cosine]])
    both = np.stack([right, right.T]).astype(np.float32)
    high = both.astype(jnp.bfloat16)
    low = (both - high.astype(np.float32)).astype(jnp.bfloat16)
    return np.stack([high, low], axis=1)


def split(value):
    high = value.astype(jnp.bfloat16)
    low = (value - high.astype(jnp.float32)).astype(jnp.bfloat16)
    return high, low


def dot(a, b):
    return lax.dot_general(a, b, (((1,), (0,)), ((), ())), preferred_element_type=jnp.float32)


def blocks(value):
    n = WIN
    return value[:n, :n], value[:n, n:], value[n:, :n], value[n:, n:]


def assemble(a, b, c, d):
    top = jnp.concatenate([a, b], axis=1)
    bottom = jnp.concatenate([c, d], axis=1)
    return jnp.concatenate([top, bottom], axis=0)


def right_product(value, w_ref, k):
    high, low = split(value)
    return dot(high, w_ref[k, 0]) + dot(low, w_ref[k, 0]) + dot(high, w_ref[k, 1])


def left_product(value, w_ref, k):
    high, low = split(value)
    return dot(w_ref[k, 0], high) + dot(w_ref[k, 0], low) + dot(w_ref[k, 1], high)


def forward(wins, probe_ref, measured, live, w_ref):
    p0r, p0i = probe_ref[0, 0], probe_ref[0, 1]
    p1r, p1i = probe_ref[1, 0], probe_ref[1, 1]
    waves = [assemble(
        p0r * a - p0i * b,
        p0r * b + p0i * a,
        p1r * a - p1i * b,
        p1r * b + p1i * a,
    ) for a, b in wins]
    xs = []
    for half in [right_product(v, w_ref, 0) for v in waves]:
        m0r, m0i, m1r, m1i = blocks(half)
        xs.append(assemble(m0r, m1r, m0i, m1i))
    out = []
    for k, far in enumerate([left_product(v, w_ref, 1) for v in xs]):
        f0r, f1r, f0i, f1i = blocks(far)
        intensity = f0r * f0r + f0i * f0i + (f1r * f1r + f1i * f1i)
        weight = live[k] - (live[k] * measured[k]) * lax.rsqrt(jnp.maximum(intensity, FLOOR))
        out.append(assemble(weight * f0r, weight * f1r, weight * f0i, weight * f1i))
    return out


def inverse(values, wins, probe_ref, w_ref):
    p0r, p0i = probe_ref[0, 0], probe_ref[0, 1]
    p1r, p1i = probe_ref[1, 0], probe_ref[1, 1]
    xs = []
    for half in [left_product(v, w_ref, 0) for v in values]:
        m0r, m1r, m0i, m1i = blocks(half)
        xs.append(assemble(m0r, m0i, m1r, m1i))
    out = []
    for (a, b), back in zip(wins, [right_product(v, w_ref, 1) for v in xs]):
        b0r, b0i, b1r, b1i = blocks(back)
        grad_re = p0r * b0r + p0i * b0i + (p1r * b1r + p1i * b1i)
        grad_im = p0r * b0i - p0i * b0r + (p1r * b1i - p1i * b1r)
        out.append((grad_re, grad_im, (a * b0r + b * b0i, a * b0i - b * b0r, a * b1r + b * b1i, a * b1i - b * b1r)))
    return out


def body(
    count_ref, place_ref, probe_ref, w_ref, tile_ref, left_ref, right_ref, top_ref, bottom_ref, corner_ref, measured_ref,
    grad_tile, grad_left, grad_right, grad_top, grad_bottom, grad_corner, probe_out,
    obj, grad, held, sides, in_sems, held_sems,
):
    rows = tile_ref.shape[1]
    cols = tile_ref.shape[2]
    tiles = cols // WIN
    count = count_ref[0, 0]
    lane = lax.broadcasted_iota(jnp.int32, (WIN, WIN), 1)

    def fetch(slot):
        return pltpu.make_async_copy(
            measured_ref.at[slot], held.at[lax.rem(slot, AHEAD)], held_sems.at[lax.rem(slot, AHEAD)]
        )

    for ahead in range(AHEAD):
        @pl.when(ahead < count)
        def _(ahead=ahead):
            fetch(jnp.int32(ahead)).start()

    last = tiles + 1
    low = RIM + rows
    middle = RIM + rows // 2
    loads = []
    for q in range(tiles):
        span = pl.ds(q * WIN, WIN)
        loads.append((tile_ref.at[:, :, span], obj.at[:, q + 1, pl.ds(RIM, rows), :]))
        loads.append((top_ref.at[:, :, span], obj.at[:, q + 1, pl.ds(0, RIM), :]))
        loads.append((bottom_ref.at[:, :, span], obj.at[:, q + 1, pl.ds(low, RIM), :]))
    for i, (q, start) in enumerate(((0, 0), (last, 0), (0, low), (last, low))):
        loads.append((corner_ref.at[i], obj.at[:, q, pl.ds(start, RIM), :]))
    loads.append((left_ref, sides.at[0]))
    loads.append((right_ref, sides.at[1]))
    loads = [pltpu.make_async_copy(a, b, in_sems.at[i]) for i, (a, b) in enumerate(loads)]
    for copy in loads:
        copy.start()
    grad[...] = jnp.zeros_like(grad)
    probe_out[...] = jnp.zeros_like(probe_out)
    for copy in loads:
        copy.wait()
    first_half = pl.ds(RIM, rows // 2)
    second_half = pl.ds(middle, rows // 2)
    for plane in range(2):
        obj[plane, 0, first_half, :] = pltpu.roll(sides[0, plane], RIM, 1)
        obj[plane, 0, second_half, :] = sides[0, plane]
        obj[plane, last, first_half, :] = sides[1, plane]
        obj[plane, last, second_half, :] = pltpu.roll(sides[1, plane], RIM, 1)
    ty, tx = lax.axis_index("ty"), lax.axis_index("tx")

    @pl.when(ty == 0)
    def _():
        obj[:, :, pl.ds(0, RIM), :] = jnp.zeros((2, tiles + 2, RIM, WIN), jnp.float32)

    @pl.when(ty == lax.axis_size("ty") - 1)
    def _():
        obj[:, :, pl.ds(low, RIM), :] = jnp.zeros((2, tiles + 2, RIM, WIN), jnp.float32)

    @pl.when(tx == 0)
    def _():
        obj[:, 0] = jnp.zeros((2, rows + WIN, WIN), jnp.float32)

    @pl.when(tx == lax.axis_size("tx") - 1)
    def _():
        obj[:, last] = jnp.zeros((2, rows + WIN, WIN), jnp.float32)


    def info_of(slot):
        safe = jnp.minimum(slot, SLOTS - 1)
        row = place_ref[safe, 0]
        col = place_ref[safe, 1]
        return row, col // WIN, lax.rem(col, WIN)

    def take(slot):
        row, q, shift = info_of(slot)
        here = pl.ds(row, WIN)
        keep = lane < WIN - shift
        window = []
        for plane in range(2):
            first = pltpu.roll(obj[plane, q, here, :], WIN - shift, 1)
            second = pltpu.roll(obj[plane, q + 1, here, :], WIN - shift, 1)
            window.append(jnp.where(keep, first, second))
        return window

    def put(slot, grad_re, grad_im):
        row, q, shift = info_of(slot)
        here = pl.ds(row, WIN)
        after = lane >= shift
        for plane, value in enumerate((grad_re, grad_im)):
            turned = pltpu.roll(value, shift, 1)
            grad[plane, q, here, :] += jnp.where(after, turned, 0.0)
            grad[plane, q + 1, here, :] += jnp.where(after, 0.0, turned)

    def run_forward(slots):
        wins = [take(s) for s in slots]
        for s in slots:
            @pl.when(s < count)
            def _():
                fetch(s).wait()
        return wins, forward(wins, probe_ref, [held[lax.rem(s, AHEAD)] for s in slots], [jnp.where(s < count, 1.0, 0.0) for s in slots], w_ref)

    def run_inverse(slots, wins, values):
        results = inverse(values, wins, probe_ref, w_ref)
        for s, (grad_re, grad_im, terms) in zip(slots, results):
            put(s, grad_re, grad_im)
        for i in range(4):
            probe_out[i // 2, i % 2] += sum(r[2][i] for r in results)

    def refill(slots):
        for s in slots:
            @pl.when(s + AHEAD < count)
            def _():
                fetch(s + AHEAD).start()

    groups = (count + U - 1) // U
    @pl.loop(0, groups)
    def _(group):
        slots = [group * U + u for u in range(U)]
        wins, values = run_forward(slots)
        run_inverse(slots, wins, values)
        refill(slots)

    stores = []
    for q in range(tiles):
        span = pl.ds(q * WIN, WIN)
        stores.append((grad.at[:, q + 1, pl.ds(RIM, rows), :], grad_tile.at[:, :, span]))
        stores.append((grad.at[:, q + 1, pl.ds(0, RIM), :], grad_top.at[:, :, span]))
        stores.append((grad.at[:, q + 1, pl.ds(low, RIM), :], grad_bottom.at[:, :, span]))
    for i, (q, start) in enumerate(((0, 0), (last, 0), (0, low), (last, low))):
        stores.append((grad.at[:, q, pl.ds(start, RIM), :], grad_corner.at[i]))
    stores.append((sides.at[0], grad_left))
    stores.append((sides.at[1], grad_right))
    stores = [pltpu.make_async_copy(a, b, in_sems.at[i]) for i, (a, b) in enumerate(stores)]
    for copy in stores[:-2]:
        copy.start()
    near = lax.broadcasted_iota(jnp.int32, (rows // 2, WIN), 1) < RIM
    for plane in range(2):
        sides[0, plane] = jnp.where(near, pltpu.roll(grad[plane, 0, first_half, :], RIM, 1), grad[plane, 0, second_half, :])
        sides[1, plane] = jnp.where(
            near, grad[plane, last, first_half, :], pltpu.roll(grad[plane, last, second_half, :], RIM, 1)
        )
    for copy in stores[-2:]:
        copy.start()
    for copy in stores:
        copy.wait()


def tile_gradient(count, places, probe, tile, halo, measured):
    planes, rows, cols = tile.shape
    tiles = cols // WIN
    f32 = jnp.float32
    smem = pl.BlockSpec(memory_space=pltpu.SMEM)
    vmem = pl.BlockSpec(memory_space=pltpu.VMEM)
    hbm = pl.BlockSpec(memory_space=pl.ANY)
    extent = (planes, tiles + 2, rows + WIN, WIN)
    copies = 3 * tiles + 6
    return pl.pallas_call(
        body,
        out_shape=(
            jax.ShapeDtypeStruct(tile.shape, f32),
            *(jax.ShapeDtypeStruct(h.shape, f32) for h in halo),
            jax.ShapeDtypeStruct(probe.shape, f32),
        ),
        in_specs=[smem, smem, vmem, vmem] + [hbm] * 7,
        out_specs=(*[hbm] * 6, vmem),
        scratch_shapes=[
            pltpu.VMEM(extent, f32),
            pltpu.VMEM(extent, f32),
            pltpu.VMEM((AHEAD, WIN, WIN), f32),
            pltpu.VMEM((2, planes, rows // 2, WIN), f32),
            pltpu.SemaphoreType.DMA((copies,)),
            pltpu.SemaphoreType.DMA((AHEAD,)),
        ],
        compiler_params=pltpu.CompilerParams(vmem_limit_bytes=48 * 1024 * 1024),
        name="tile_gradient",
    )(count, places, probe, jnp.asarray(matrices()), tile, *halo, measured)


AROUND = ((-1, 0), (1, 0), (0, -1), (0, 1), (-1, -1), (-1, 1), (1, -1), (1, 1))


def ring(axis, by):
    size = lax.axis_size(axis)
    return lax.rem(lax.axis_index(axis) + (by + size), size)


def around(dy, dx):
    return {"ty": ring("ty", dy), "tx": ring("tx", dx)}


def greet(partners):
    barrier = pltpu.get_barrier_semaphore()
    for partner in partners:
        pl.semaphore_signal(barrier, inc=1, device_id=partner, device_id_type=MESH)


def halo_body(
    tile_ref, left_out, right_out, top_out, bottom_out, corner_out, edge, packed, in_sems, send_sems, recv_sems
):
    rows, cols = tile_ref.shape[1:]
    greet([around(*step) for step in AROUND])
    firsts = pltpu.make_async_copy(tile_ref.at[:, :, pl.ds(0, WIN)], edge.at[0], in_sems.at[0])
    lasts = pltpu.make_async_copy(tile_ref.at[:, :, pl.ds(cols - WIN, WIN)], edge.at[1], in_sems.at[1])
    firsts.start()
    lasts.start()
    half = rows // 2
    near = lax.broadcasted_iota(jnp.int32, (half, WIN), 1) < RIM
    firsts.wait()
    for plane in range(2):
        packed[0, plane] = jnp.where(
            near, edge[0, plane, pl.ds(0, half), :], pltpu.roll(edge[0, plane, pl.ds(half, half), :], RIM, 1)
        )
    lasts.wait()
    for plane in range(2):
        packed[1, plane] = jnp.where(
            near, pltpu.roll(edge[1, plane, pl.ds(0, half), :], RIM, 1), edge[1, plane, pl.ds(half, half), :]
        )
    pl.semaphore_wait(pltpu.get_barrier_semaphore(), len(AROUND))
    above, below = pl.ds(0, RIM), pl.ds(rows - RIM, RIM)
    start, stop = pl.ds(0, WIN), pl.ds(cols - WIN, WIN)
    moves = (
        (packed.at[0], right_out, (0, -1)),
        (packed.at[1], left_out, (0, 1)),
        (tile_ref.at[:, above, :], bottom_out, (-1, 0)),
        (tile_ref.at[:, below, :], top_out, (1, 0)),
        (tile_ref.at[:, below, stop], corner_out.at[0], (1, 1)),
        (tile_ref.at[:, below, start], corner_out.at[1], (1, -1)),
        (tile_ref.at[:, above, stop], corner_out.at[2], (-1, 1)),
        (tile_ref.at[:, above, start], corner_out.at[3], (-1, -1)),
    )
    send(moves, send_sems, recv_sems)


def send(moves, send_sems, recv_sems, wait=True):
    copies = [
        pltpu.make_async_remote_copy(
            src_ref=source,
            dst_ref=target,
            send_sem=send_sems.at[i],
            recv_sem=recv_sems.at[i],
            device_id=around(*step),
            device_id_type=MESH,
        )
        for i, (source, target, step) in enumerate(moves)
    ]
    for copy in copies:
        copy.start()
    if wait:
        for copy in copies:
            copy.wait()
    return copies


def halo_shapes(tile):
    planes, rows, cols = tile.shape
    shapes = [(planes, rows // 2, WIN)] * 2 + [(planes, RIM, cols)] * 2 + [(4, planes, RIM, WIN)]
    return tuple(jax.ShapeDtypeStruct(s, jnp.float32) for s in shapes)


def gather_halo(tile):
    planes, rows, cols = tile.shape
    hbm = pl.BlockSpec(memory_space=pl.ANY)
    return pl.pallas_call(
        halo_body,
        out_shape=halo_shapes(tile),
        in_specs=[hbm],
        out_specs=(hbm,) * 5,
        scratch_shapes=[
            pltpu.VMEM((2, planes, rows, WIN), jnp.float32),
            pltpu.VMEM((2, planes, rows // 2, WIN), jnp.float32),
            pltpu.SemaphoreType.DMA((2,)),
            pltpu.SemaphoreType.DMA((8,)),
            pltpu.SemaphoreType.DMA((8,)),
        ],
        compiler_params=pltpu.CompilerParams(
            collective_id=0, has_side_effects=True, vmem_limit_bytes=16 * 1024 * 1024
        ),
        name="gather_halo",
    )(tile)


def tail_body(
    left_ref, right_ref, top_ref, bottom_ref, corner_ref, part_ref,
    left_out, right_out, top_out, bottom_out, corner_out, total_out,
    gathered, stage, send_sems, recv_sems, tx_send, tx_recv, ty_send, ty_recv, out_send, out_recv,
):
    ty, tx = lax.axis_index("ty"), lax.axis_index("tx")
    ny, nx = lax.axis_size("ty"), lax.axis_size("tx")
    diagonal = [around(*step) for step in AROUND if 0 not in step]
    greet(diagonal)
    barrier = pltpu.get_barrier_semaphore()

    @pl.loop(1, nx)
    def _(k):
        pl.semaphore_signal(barrier, inc=1, device_id={"tx": lax.rem(tx + k, nx)}, device_id_type=MESH)

    @pl.loop(1, ny)
    def _(k):
        pl.semaphore_signal(barrier, inc=1, device_id={"ty": lax.rem(ty + k, ny)}, device_id_type=MESH)

    pl.semaphore_wait(barrier, len(diagonal) + nx - 1 + ny - 1)

    def to_column(k, source, target, sends, receives):
        return pltpu.make_async_remote_copy(
            src_ref=source,
            dst_ref=target,
            send_sem=sends.at[k],
            recv_sem=receives.at[tx],
            device_id={"tx": lax.rem(tx + k, nx)},
            device_id_type=MESH,
        )

    def to_row(k):
        return pltpu.make_async_remote_copy(
            src_ref=stage.at[ty],
            dst_ref=stage.at[ty],
            send_sem=ty_send.at[k],
            recv_sem=ty_recv.at[ty],
            device_id={"ty": lax.rem(ty + k, ny)},
            device_id_type=MESH,
        )

    def arrived(target, semaphore):
        pltpu.make_async_copy(target, target, semaphore).wait()

    def spread(k):
        return to_column(k, part_ref.at[lax.rem(tx + k, nx)], gathered.at[tx], tx_send, tx_recv)

    def share(k):
        return to_column(k, total_out.at[tx], total_out.at[tx], out_send, out_recv)

    @pl.loop(1, nx)
    def _(k):
        spread(k).start()

    moves = (
        (left_ref, right_out, (0, -1)),
        (right_ref, left_out, (0, 1)),
        (top_ref, bottom_out, (-1, 0)),
        (bottom_ref, top_out, (1, 0)),
        (corner_ref.at[0], corner_out.at[3], (-1, -1)),
        (corner_ref.at[1], corner_out.at[2], (-1, 1)),
        (corner_ref.at[2], corner_out.at[1], (1, -1)),
        (corner_ref.at[3], corner_out.at[0], (1, 1)),
    )
    halo = send(moves, send_sems, recv_sems, wait=False)

    stage[ty] = part_ref[tx]

    @pl.loop(1, nx)
    def _(k):
        source = lax.rem(tx + k, nx)
        arrived(gathered.at[source], tx_recv.at[source])
        stage[ty] += gathered[source]

    @pl.loop(1, ny)
    def _(k):
        to_row(k).start()

    @pl.loop(1, ny)
    def _(k):
        source = lax.rem(ty + k, ny)
        arrived(stage.at[source], ty_recv.at[source])

    total = stage[0]
    for i in range(1, stage.shape[0]):
        total += stage[i]
    total_out[tx] = total * (1.0 / SLOTS_ALL)

    @pl.loop(1, nx)
    def _(k):
        share(k).start()

    @pl.loop(1, nx)
    def _(k):
        source = lax.rem(tx + k, nx)
        arrived(total_out.at[source], out_recv.at[source])

    for copy in halo:
        copy.wait()

    @pl.loop(1, nx)
    def _(k):
        spread(k).wait_send()
        share(k).wait_send()

    @pl.loop(1, ny)
    def _(k):
        to_row(k).wait_send()


def exchange(halo, part):
    hbm = pl.BlockSpec(memory_space=pl.ANY)
    vmem = pl.BlockSpec(memory_space=pltpu.VMEM)
    ny, nx = lax.axis_size("ty"), lax.axis_size("tx")
    chunk = (part.size // (nx * WIN), WIN)
    return pl.pallas_call(
        tail_body,
        out_shape=(
            *(jax.ShapeDtypeStruct(h.shape, jnp.float32) for h in halo),
            jax.ShapeDtypeStruct((nx, *chunk), jnp.float32),
        ),
        in_specs=[hbm] * 5 + [vmem],
        out_specs=(*[hbm] * 5, vmem),
        scratch_shapes=[
            pltpu.VMEM((nx, *chunk), jnp.float32),
            pltpu.VMEM((ny, *chunk), jnp.float32),
            pltpu.SemaphoreType.DMA((8,)),
            pltpu.SemaphoreType.DMA((8,)),
            pltpu.SemaphoreType.DMA((nx,)),
            pltpu.SemaphoreType.DMA((nx,)),
            pltpu.SemaphoreType.DMA((ny,)),
            pltpu.SemaphoreType.DMA((ny,)),
            pltpu.SemaphoreType.DMA((nx,)),
            pltpu.SemaphoreType.DMA((nx,)),
        ],
        compiler_params=pltpu.CompilerParams(
            collective_id=1, has_side_effects=True, vmem_limit_bytes=16 * 1024 * 1024
        ),
        name="exchange",
    )(*halo, part.reshape(nx, *chunk))


def finish_body(
    tile_ref, left_ref, right_ref, top_ref, bottom_ref, corner_ref, total_ref, out_ref, total_out, edge, strip, in_sems
):
    planes, rows, cols = tile_ref.shape
    ty, tx = lax.axis_index("ty"), lax.axis_index("tx")
    ny, nx = lax.axis_size("ty"), lax.axis_size("tx")
    half = rows // 2
    ends = (pl.ds(0, RIM), pl.ds(rows - RIM, RIM))
    sides = (pl.ds(0, WIN), pl.ds(cols - WIN, WIN))
    inner = pl.ds(WIN, cols - 2 * WIN)
    parts = [(out_ref.at[:, :, span], edge.at[i]) for i, span in enumerate(sides)]
    parts += [(out_ref.at[:, span, inner], strip.at[i]) for i, span in enumerate(ends)]
    reads = [pltpu.make_async_copy(a, b, in_sems.at[i]) for i, (a, b) in enumerate(parts)]
    for copy in reads:
        copy.start()
    total_out[...] = total_ref[...]
    lane = lax.broadcasted_iota(jnp.int32, (half, WIN), 1)
    near = lane < RIM
    lane = lane[:RIM]
    no_side = (tx == 0, tx == nx - 1)
    no_end = (ty == 0, ty == ny - 1)
    for copy in reads:
        copy.wait()
    for plane in range(2):
        for i, packed in enumerate((left_ref, right_ref)):
            value = jnp.where(no_side[i], 0.0, packed[plane])
            turned = pltpu.roll(value, RIM, 1)
            mine = near if i == 0 else jnp.logical_not(near)
            first, second = (value, turned) if i == 0 else (turned, value)
            edge[i, plane, pl.ds(0, half), :] += jnp.where(mine, first, 0.0)
            edge[i, plane, pl.ds(half, half), :] += jnp.where(mine, second, 0.0)
        for j, rim in enumerate((top_ref, bottom_ref)):
            for i in range(2):
                value = jnp.where(no_end[j], 0.0, rim[plane, :, sides[i]])
                gone = jnp.logical_or(no_side[i], no_end[j])
                value += jnp.where(gone, 0.0, corner_ref[2 * j + i, plane])
                edge[i, plane, ends[j], :] += value
            strip[j, plane] += jnp.where(no_end[j], 0.0, rim[plane, :, inner])
    writes = [pltpu.make_async_copy(b, a, in_sems.at[i]) for i, (a, b) in enumerate(parts)]
    for copy in writes:
        copy.start()
    for copy in writes:
        copy.wait()


def finish(tile, halo, total):
    planes, rows, cols = tile.shape
    hbm = pl.BlockSpec(memory_space=pl.ANY)
    vmem = pl.BlockSpec(memory_space=pltpu.VMEM)
    return pl.pallas_call(
        finish_body,
        out_shape=(jax.ShapeDtypeStruct(tile.shape, jnp.float32), jax.ShapeDtypeStruct(total.shape, jnp.float32)),
        in_specs=[hbm] + [vmem] * 6,
        out_specs=(hbm, vmem),
        scratch_shapes=[
            pltpu.VMEM((2, planes, rows, WIN), jnp.float32),
            pltpu.VMEM((2, planes, RIM, cols - 2 * WIN), jnp.float32),
            pltpu.SemaphoreType.DMA((4,)),
        ],
        input_output_aliases={0: 0},
        compiler_params=pltpu.CompilerParams(vmem_limit_bytes=16 * 1024 * 1024),
        name="finish",
    )(tile, *halo, total)


def shards(object_planes, probe, positions, counts, amplitudes):
    planes, rows, cols = object_planes.shape
    halo = gather_halo(object_planes)
    base = jnp.stack([lax.axis_index("ty") * rows - RIM, lax.axis_index("tx") * cols - WIN]).astype(jnp.int32)
    places = positions[0, 0] - base
    tile, *outer, part = tile_gradient(counts, places, probe, object_planes, halo, amplitudes[0, 0])
    *outer, total = exchange(outer, part)
    tile, total = finish(tile, outer, total)
    return tile, total.reshape(probe.shape)


def solution(mesh):
    in_specs = (
        P(None, "ty", "tx"),
        P(),
        P("ty", "tx", None, None),
        P("ty", "tx"),
        P("ty", "tx", None, None, None),
    )
    out_specs = (P(None, "ty", "tx"), P())
    return jax.shard_map(shards, mesh=mesh, in_specs=in_specs, out_specs=out_specs, check_vma=False)
```

time: 386 us -> 146 us (0.38)
  waiting for transfers between devices: 266 us -> 0 us
  Pallas kernels: 27.3 us -> 141 us
  starting transfers between devices: 36.1 us -> 0 us
  local copies, waits for them, and re-layouts: 30.8 us -> 2.97 us
  between operations: 15.1 us -> 1.33 us
  other arithmetic: 8.39 us -> 0.08 us
    psum x1 -> x0, waiting for transfers between devices: 254 us -> none  [shards(): total = lax.psum(probe_part, ('ty', 'tx'))]
    pallas_call x1 -> x4, Pallas kernels: 27.3 us -> 141 us  [the longest x1 93.5 us: exchange(): pl.pallas_call(tail_body, out_shape=(*(jax.ShapeDtypeStruct(h.shape, jnp....]
    ppermute x8 -> x0, starting transfers between devices: 36 us -> none  [shifted(): return lax.ppermute(value, axis, pairs)]
    scatter-add x6 -> x0, local copies, waits for them, and re-layouts: 14 us -> none  [the longest x1 5.95 us: shards(): out = g_tile.at[:, :, cols - RIM:].add(from_right[:, RIM:RIM + rows])]
    ppermute x8 -> x0, waiting for transfers between devices: 12.1 us -> none  [shifted(): return lax.ppermute(value, axis, pairs)]
    slice x15 -> x0, local copies, waits for them, and re-layouts: 7.45 us -> none  [the longest x1 1.9 us: shards(): object_planes[:, :, :RIM]]
  transfers between devices with their start and end apart: 9 -> 0, of which waited for: 4 -> 0; matrix products, arithmetic and copies ran while one was open for 8% -> 0% of each run, Pallas kernels for 0% -> 0%
where the time goes in v2:
time: 146 us
  Pallas kernels  141 us (97%)
  local copies, waits for them, and re-layouts  2.97 us (2%)
    pallas_call x1, Pallas kernels, exchange(): pl.pallas_call(tail_body, out_shape=(*(jax.ShapeDtypeStruct(h.shape, jnp....  93.5 us
    pallas_call x1, Pallas kernels, gather_halo(): pl.pallas_call(halo_body, out_shape=halo_shapes(tile), in_specs=[hbm], ou...  32.6 us
    pallas_call x1, Pallas kernels, tile_gradient(): pl.pallas_call(body, out_shape=(jax.ShapeDtypeStruct(tile.shape, f32), *(...  11.1 us
    pallas_call x1, Pallas kernels, finish(): pl.pallas_call(finish_body, out_shape=(jax.ShapeDtypeStruct(tile.shape, j...  4.09 us
    unnamed x7, local copies, waits for them, and re-layouts  2.97 us

profile of v2, /device:TPU:1, one launch (start us, length us, event | category | flops | bytes accessed | tf_op | source)
XLA Modules:
  0.0 145.7 jit_solution(10116443694509141059)
XLA Ops:
  1.3 0.1 pad_add_fusion
  1.4 0.8 copy.9
  2.1 0.0 copy-start
  2.2 2.2 %copy-done = f32[2,1024,512]{2,1,0:T(8,128)S(1)} copy-done((f32[2,1024,512]{2,1,0:T(8,128)S(1)}, f32[2,1024,512]{2,1,0:T(8,128)}, u32[]{:S(2)}) %copy-start) | copy-done | bytes 4194328
  4.3 0.0 copy-start.1
  4.3 0.0 copy-start.2
  4.3 32.6 %gather_halo.1 = (f32[2,512,128]{2,1,0:T(8,128)S(1)}, f32[2,512,128]{2,1,0:T(8,128)S(1)}, f32[2,64,512]{2,1,0:T(8,128)S(1)}, f32[2,64,512]{2,1,0:T(8,128)S(1)}, f32[4,2,64,128]{3,2,1,0:T(8,128)S(1)}) custom-call(f32[2,1024,512]{2,1,0:T(8,128)S(1)} %copy-done), custom_call_target="tpu_custom_call" | custom-call | tf_op jit(solution)/shard_map/gather_halo/pallas_call | solution.py:364
  37.0 0.0 copy-done.1
  37.0 0.0 copy-done.2
  37.0 11.1 %tile_gradient.1 = (f32[2,1024,512]{2,1,0:T(8,128)}, f32[2,512,128]{2,1,0:T(8,128)S(1)}, f32[2,512,128]{2,1,0:T(8,128)S(1)}, f32[2,64,512]{2,1,0:T(8,128)S(1)}, ...) custom-call(s32[1,1]{1,0:T(1,128)S(6)} %copy.11.count_ref, ...), custom_call_target="tpu_custom_call" | custom-call | tf_op jit(solution)/shard_map/tile_gradient/pallas_call | solution.py:258
  48.1 93.5 %exchange.1 = (f32[2,512,128]{2,1,0:T(8,128)S(1)}, f32[2,512,128]{2,1,0:T(8,128)S(1)}, f32[2,64,512]{2,1,0:T(8,128)S(1)}, f32[2,64,512]{2,1,0:T(8,128)S(1)}, f32...) custom-call(f32[2,512,128]{2,1,0:T(8,128)S(1)} %get-tuple-element.28.left_ref, ...), custom_call_target="tpu_custom_call" | custom-call | tf_op jit(solution)/shard_map/exchange/pallas_call | solution.py:498
  141.6 4.1 %finish.1 = (f32[2,1024,512]{2,1,0:T(8,128)}, f32[16,32,128]{2,1,0:T(8,128)}) custom-call(f32[2,1024,512]{2,1,0:T(8,128)} %get-tuple-element.27.tile_ref, f32[2,512,128]{2,1,0:T(8,128)S(1)} %get-tuple-element.34.left_ref, f32[2,512,128]{2,1,0:T(8,128)S(1)} %get-tuple-element.35.right_ref, ...), custom_call_target="tpu_custom_call", output_to_operand_aliasing={{0}: (0, {})} | custom-call | tf_op jit(solution)/shard_map/finish/pallas_call | solution.py:574
  (1 shorter events, 0.0 us)
Async XLA Ops:
  2.1 2.2 %copy-start = (f32[2,1024,512]{2,1,0:T(8,128)S(1)}, f32[2,1024,512]{2,1,0:T(8,128)}, u32[]{:S(2)}) copy-start(f32[2,1024,512]{2,1,0:T(8,128)} %tile_ref.3) | copy-start | bytes 12582916
  4.3 32.6 %copy-start.1 = (bf16[2,2,256,256]{3,2,1,0:T(8,128)(2,1)S(1)}, bf16[2,2,256,256]{3,2,1,0:T(8,128)(2,1)}, u32[]{:S(2)}) copy-start(bf16[2,2,256,256]{3,2,1,0:T(8,128)(2,1)} %constant.21.clone.w_ref) | copy-start | bytes 1572868
  4.3 32.7 %copy-start.2 = (f32[2,2,128,128]{3,2,1,0:T(8,128)S(1)}, f32[2,2,128,128]{3,2,1,0:T(8,128)}, u32[]{:S(2)}) copy-start(f32[2,2,128,128]{3,2,1,0:T(8,128)} %probe_ref.1) | copy-start | bytes 786436

commit v3 on v2

--- a/solution.py
+++ b/solution.py
@@ -15,7 +15,7 @@
 MESH = pl.DeviceIdType.MESH
 SLOTS_ALL = 8 * 16 * 96
 U = 8
-SLOTS = 96
+EARLY = 48
 
 
 def matrices():
@@ -99,26 +99,46 @@
     return out
 
 
+def take(obj, row, q, q_next, shift):
+    here = pl.ds(row, WIN)
+    keep = lax.broadcasted_iota(jnp.int32, (WIN, WIN), 1) < WIN - shift
+    window = []
+    for plane in range(2):
+        first = pltpu.roll(obj[plane, q, here, :], WIN - shift, 1)
+        second = pltpu.roll(obj[plane, q_next, here, :], WIN - shift, 1)
+        window.append(jnp.where(keep, first, second))
+    return window
+
+
+def put(grad, row, q, shift, values):
+    here = pl.ds(row, WIN)
+    after = lax.broadcasted_iota(jnp.int32, (WIN, WIN), 1) >= shift
+    for plane, value in enumerate(values):
+        turned = pltpu.roll(value, shift, 1)
+        grad[plane, q, here, :] += jnp.where(after, turned, 0.0)
+        grad[plane, q + 1, here, :] += jnp.where(after, 0.0, turned)
+
+
 def body(
-    count_ref, place_ref, probe_ref, w_ref, tile_ref, left_ref, right_ref, top_ref, bottom_ref, corner_ref, measured_ref,
+    place_ref, number_ref, probe_ref, w_ref, tile_ref, left_ref, right_ref, top_ref, bottom_ref, corner_ref,
+    measured_ref, patch_ref, part_ref,
     grad_tile, grad_left, grad_right, grad_top, grad_bottom, grad_corner, probe_out,
-    obj, grad, held, sides, in_sems, held_sems,
+    obj, grad, held, sides, patches, in_sems, held_sems, patch_sem,
 ):
     rows = tile_ref.shape[1]
     cols = tile_ref.shape[2]
     tiles = cols // WIN
-    count = count_ref[0, 0]
-    lane = lax.broadcasted_iota(jnp.int32, (WIN, WIN), 1)
-
-    def fetch(slot):
-        return pltpu.make_async_copy(
-            measured_ref.at[slot], held.at[lax.rem(slot, AHEAD)], held_sems.at[lax.rem(slot, AHEAD)]
-        )
+    begin, count = number_ref[0], number_ref[1]
+    slots_max = place_ref.shape[1]
+
+    def fetch(place):
+        turn = lax.rem(place - begin, AHEAD)
+        return pltpu.make_async_copy(measured_ref.at[place_ref[0, place]], held.at[turn], held_sems.at[turn])
 
     for ahead in range(AHEAD):
-        @pl.when(ahead < count)
+        @pl.when(begin + ahead < count)
         def _(ahead=ahead):
-            fetch(jnp.int32(ahead)).start()
+            fetch(begin + ahead).start()
 
     last = tiles + 1
     low = RIM + rows
@@ -134,10 +154,12 @@
     loads.append((left_ref, sides.at[0]))
     loads.append((right_ref, sides.at[1]))
     loads = [pltpu.make_async_copy(a, b, in_sems.at[i]) for i, (a, b) in enumerate(loads)]
+    early = pltpu.make_async_copy(patch_ref, patches, patch_sem)
+    early.start()
     for copy in loads:
         copy.start()
     grad[...] = jnp.zeros_like(grad)
-    probe_out[...] = jnp.zeros_like(probe_out)
+    probe_out[...] = part_ref[...]
     for copy in loads:
         copy.wait()
     first_half = pl.ds(RIM, rows // 2)
@@ -166,60 +188,39 @@
         obj[:, last] = jnp.zeros((2, rows + WIN, WIN), jnp.float32)
 
 
-    def info_of(slot):
-        safe = jnp.minimum(slot, SLOTS - 1)
-        row = place_ref[safe, 0]
-        col = place_ref[safe, 1]
+    def info_of(place):
+        safe = jnp.minimum(place, slots_max - 1)
+        row, col = place_ref[1, safe], place_ref[2, safe]
         return row, col // WIN, lax.rem(col, WIN)
 
-    def take(slot):
-        row, q, shift = info_of(slot)
-        here = pl.ds(row, WIN)
-        keep = lane < WIN - shift
-        window = []
-        for plane in range(2):
-            first = pltpu.roll(obj[plane, q, here, :], WIN - shift, 1)
-            second = pltpu.roll(obj[plane, q + 1, here, :], WIN - shift, 1)
-            window.append(jnp.where(keep, first, second))
-        return window
-
-    def put(slot, grad_re, grad_im):
-        row, q, shift = info_of(slot)
-        here = pl.ds(row, WIN)
-        after = lane >= shift
-        for plane, value in enumerate((grad_re, grad_im)):
-            turned = pltpu.roll(value, shift, 1)
-            grad[plane, q, here, :] += jnp.where(after, turned, 0.0)
-            grad[plane, q + 1, here, :] += jnp.where(after, 0.0, turned)
-
-    def run_forward(slots):
-        wins = [take(s) for s in slots]
-        for s in slots:
-            @pl.when(s < count)
+    early.wait()
+
+    @pl.loop(0, begin)
+    def _(place):
+        put(grad, *info_of(place), (patches[place, 0], patches[place, 1]))
+
+    @pl.loop(0, (count - begin + U - 1) // U)
+    def _(group):
+        places = [begin + group * U + u for u in range(U)]
+        wins = []
+        for place in places:
+            row, q, shift = info_of(place)
+            wins.append(take(obj, row, q, q + 1, shift))
+        for place in places:
+            @pl.when(place < count)
             def _():
-                fetch(s).wait()
-        return wins, forward(wins, probe_ref, [held[lax.rem(s, AHEAD)] for s in slots], [jnp.where(s < count, 1.0, 0.0) for s in slots], w_ref)
-
-    def run_inverse(slots, wins, values):
-        results = inverse(values, wins, probe_ref, w_ref)
-        for s, (grad_re, grad_im, terms) in zip(slots, results):
-            put(s, grad_re, grad_im)
+                fetch(place).wait()
+        held_now = [held[lax.rem(place - begin, AHEAD)] for place in places]
+        live = [jnp.where(place < count, 1.0, 0.0) for place in places]
+        results = inverse(forward(wins, probe_ref, held_now, live, w_ref), wins, probe_ref, w_ref)
+        for place, (grad_re, grad_im, terms) in zip(places, results):
+            put(grad, *info_of(place), (grad_re, grad_im))
         for i in range(4):
             probe_out[i // 2, i % 2] += sum(r[2][i] for r in results)
-
-    def refill(slots):
-        for s in slots:
-            @pl.when(s + AHEAD < count)
+        for place in places:
+            @pl.when(place + AHEAD < count)
             def _():
-                fetch(s + AHEAD).start()
-
-    groups = (count + U - 1) // U
-    @pl.loop(0, groups)
-    def _(group):
-        slots = [group * U + u for u in range(U)]
-        wins, values = run_forward(slots)
-        run_inverse(slots, wins, values)
-        refill(slots)
+                fetch(place + AHEAD).start()
 
     stores = []
     for q in range(tiles):
@@ -246,7 +247,7 @@
         copy.wait()
 
 
-def tile_gradient(count, places, probe, tile, halo, measured):
+def tile_gradient(places, numbers, probe, tile, halo, measured, patches, part):
     planes, rows, cols = tile.shape
     tiles = cols // WIN
     f32 = jnp.float32
@@ -262,19 +263,21 @@
             *(jax.ShapeDtypeStruct(h.shape, f32) for h in halo),
             jax.ShapeDtypeStruct(probe.shape, f32),
         ),
-        in_specs=[smem, smem, vmem, vmem] + [hbm] * 7,
+        in_specs=[smem, smem, vmem, vmem] + [hbm] * 8 + [vmem],
         out_specs=(*[hbm] * 6, vmem),
         scratch_shapes=[
             pltpu.VMEM(extent, f32),
             pltpu.VMEM(extent, f32),
             pltpu.VMEM((AHEAD, WIN, WIN), f32),
             pltpu.VMEM((2, planes, rows // 2, WIN), f32),
+            pltpu.VMEM(patches.shape, f32),
             pltpu.SemaphoreType.DMA((copies,)),
             pltpu.SemaphoreType.DMA((AHEAD,)),
+            pltpu.SemaphoreType.DMA,
         ],
-        compiler_params=pltpu.CompilerParams(vmem_limit_bytes=48 * 1024 * 1024),
+        compiler_params=pltpu.CompilerParams(vmem_limit_bytes=56 * 1024 * 1024),
         name="tile_gradient",
-    )(count, places, probe, jnp.asarray(matrices()), tile, *halo, measured)
+    )(places, numbers, probe, jnp.asarray(matrices()), tile, *halo, measured, patches, part)
 
 
 AROUND = ((-1, 0), (1, 0), (0, -1), (0, 1), (-1, -1), (-1, 1), (1, -1), (1, 1))
@@ -296,25 +299,32 @@
 
 
 def halo_body(
-    tile_ref, left_out, right_out, top_out, bottom_out, corner_out, edge, packed, in_sems, send_sems, recv_sems
+    place_ref, live_ref, probe_ref, w_ref, tile_ref, measured_ref,
+    left_out, right_out, top_out, bottom_out, corner_out, patch_out, part_out,
+    obj, held, packed, patches, in_sems, held_sem, send_sems, recv_sems, patch_sems,
 ):
     rows, cols = tile_ref.shape[1:]
+    tiles = cols // WIN
     greet([around(*step) for step in AROUND])
-    firsts = pltpu.make_async_copy(tile_ref.at[:, :, pl.ds(0, WIN)], edge.at[0], in_sems.at[0])
-    lasts = pltpu.make_async_copy(tile_ref.at[:, :, pl.ds(cols - WIN, WIN)], edge.at[1], in_sems.at[1])
-    firsts.start()
-    lasts.start()
+    loads = [
+        pltpu.make_async_copy(tile_ref.at[:, :, pl.ds(q * WIN, WIN)], obj.at[:, q], in_sems.at[q])
+        for q in range(tiles)
+    ]
+    for q in (0, tiles - 1, *range(1, tiles - 1)):
+        loads[q].start()
+    measures = pltpu.make_async_copy(measured_ref, held, held_sem)
+    measures.start()
+    part_out[...] = jnp.zeros_like(part_out)
     half = rows // 2
+    first, second = pl.ds(0, half), pl.ds(half, half)
     near = lax.broadcasted_iota(jnp.int32, (half, WIN), 1) < RIM
-    firsts.wait()
+    loads[0].wait()
     for plane in range(2):
-        packed[0, plane] = jnp.where(
-            near, edge[0, plane, pl.ds(0, half), :], pltpu.roll(edge[0, plane, pl.ds(half, half), :], RIM, 1)
-        )
-    lasts.wait()
+        packed[0, plane] = jnp.where(near, obj[plane, 0, first, :], pltpu.roll(obj[plane, 0, second, :], RIM, 1))
+    loads[tiles - 1].wait()
     for plane in range(2):
         packed[1, plane] = jnp.where(
-            near, pltpu.roll(edge[1, plane, pl.ds(0, half), :], RIM, 1), edge[1, plane, pl.ds(half, half), :]
+            near, pltpu.roll(obj[plane, tiles - 1, first, :], RIM, 1), obj[plane, tiles - 1, second, :]
         )
     pl.semaphore_wait(pltpu.get_barrier_semaphore(), len(AROUND))
     above, below = pl.ds(0, RIM), pl.ds(rows - RIM, RIM)
@@ -329,7 +339,43 @@
         (tile_ref.at[:, above, stop], corner_out.at[2], (-1, 1)),
         (tile_ref.at[:, above, start], corner_out.at[3], (-1, -1)),
     )
-    send(moves, send_sems, recv_sems)
+    halo = send(moves, send_sems, recv_sems, wait=False)
+    for q in range(1, tiles - 1):
+        loads[q].wait()
+    measures.wait()
+
+    def store(group):
+        turn = lax.rem(group, 2)
+        return pltpu.make_async_copy(patches.at[turn], patch_out.at[pl.ds(group * U, U)], patch_sems.at[turn])
+
+    groups = patch_out.shape[0] // U
+
+    @pl.loop(0, groups)
+    def _(group):
+        turn = lax.rem(group, 2)
+
+        @pl.when(group >= 2)
+        def _():
+            store(group - 2).wait()
+
+        places = [group * U + u for u in range(U)]
+        wins = [
+            take(obj, place_ref[3, p], place_ref[4, p], place_ref[5, p], place_ref[6, p]) for p in places
+        ]
+        held_now = [held[place_ref[0, p]] for p in places]
+        live = [live_ref[p] for p in places]
+        results = inverse(forward(wins, probe_ref, held_now, live, w_ref), wins, probe_ref, w_ref)
+        for u, (grad_re, grad_im, terms) in enumerate(results):
+            patches[turn, u, 0] = grad_re
+            patches[turn, u, 1] = grad_im
+        for i in range(4):
+            part_out[i // 2, i % 2] += sum(r[2][i] for r in results)
+        store(group).start()
+
+    for group in range(max(groups - 2, 0), groups):
+        store(group).wait()
+    for copy in halo:
+        copy.wait()
 
 
 def send(moves, send_sems, recv_sems, wait=True):
@@ -358,26 +404,58 @@
     return tuple(jax.ShapeDtypeStruct(s, jnp.float32) for s in shapes)
 
 
-def gather_halo(tile):
+def gather_halo(places, live, probe, tile, measured):
     planes, rows, cols = tile.shape
     hbm = pl.BlockSpec(memory_space=pl.ANY)
+    smem = pl.BlockSpec(memory_space=pltpu.SMEM)
+    vmem = pl.BlockSpec(memory_space=pltpu.VMEM)
+    f32 = jnp.float32
     return pl.pallas_call(
         halo_body,
-        out_shape=halo_shapes(tile),
-        in_specs=[hbm],
-        out_specs=(hbm,) * 5,
+        out_shape=(
+            *halo_shapes(tile),
+            jax.ShapeDtypeStruct((EARLY, planes, WIN, WIN), f32),
+            jax.ShapeDtypeStruct(probe.shape, f32),
+        ),
+        in_specs=[smem, smem, vmem, vmem, hbm, hbm],
+        out_specs=(*[hbm] * 6, vmem),
         scratch_shapes=[
-            pltpu.VMEM((2, planes, rows, WIN), jnp.float32),
-            pltpu.VMEM((2, planes, rows // 2, WIN), jnp.float32),
-            pltpu.SemaphoreType.DMA((2,)),
+            pltpu.VMEM((planes, cols // WIN, rows, WIN), f32),
+            pltpu.VMEM(measured.shape, f32),
+            pltpu.VMEM((2, planes, rows // 2, WIN), f32),
+            pltpu.VMEM((2, U, planes, WIN, WIN), f32),
+            pltpu.SemaphoreType.DMA((cols // WIN,)),
+            pltpu.SemaphoreType.DMA,
             pltpu.SemaphoreType.DMA((8,)),
             pltpu.SemaphoreType.DMA((8,)),
+            pltpu.SemaphoreType.DMA((2,)),
         ],
         compiler_params=pltpu.CompilerParams(
-            collective_id=0, has_side_effects=True, vmem_limit_bytes=16 * 1024 * 1024
+            collective_id=0, has_side_effects=True, vmem_limit_bytes=56 * 1024 * 1024
         ),
         name="gather_halo",
-    )(tile)
+    )(places, live, probe, jnp.asarray(matrices()), tile, measured)
+
+
+def ordered(positions, count, rows, cols):
+    slots = positions.shape[0]
+    row = positions[:, 0] - lax.axis_index("ty") * rows
+    col = positions[:, 1] - lax.axis_index("tx") * cols
+    slot = jnp.arange(slots, dtype=jnp.int32)
+    inside = (row >= 0) & (row <= rows - WIN) & (col >= 0) & (col <= cols - WIN)
+    key = jnp.where(slot < count, jnp.where(inside, 0, 1), 2) * slots + slot
+    rank = jnp.sum((key[None, :] < key[:, None]).astype(jnp.int32), axis=1)
+    safe_row = jnp.clip(row, 0, rows - WIN)
+    safe_col = jnp.clip(col, 0, cols - WIN)
+    q = safe_col // WIN
+    table = jnp.stack(
+        [slot, row + RIM, col + WIN, safe_row, q, jnp.minimum(q + 1, cols // WIN - 1), safe_col % WIN, slot * 0]
+    )
+    hit = rank[None, :] == slot[:, None]
+    table = jnp.sum(jnp.where(hit[None], table[:, None, :], 0), axis=2)
+    inner = jnp.sum((inside & (slot < count)).astype(jnp.int32))
+    live = (slot < inner).astype(jnp.float32)
+    return table, live, jnp.stack([jnp.minimum(inner, EARLY), count])
 
 
 def tail_body(
@@ -516,7 +594,7 @@
             pltpu.SemaphoreType.DMA((nx,)),
         ],
         compiler_params=pltpu.CompilerParams(
-            collective_id=1, has_side_effects=True, vmem_limit_bytes=16 * 1024 * 1024
+            collective_id=1, has_side_effects=True, vmem_limit_bytes=56 * 1024 * 1024
         ),
         name="exchange",
     )(*halo, part.reshape(nx, *chunk))
@@ -582,17 +660,17 @@
             pltpu.SemaphoreType.DMA((4,)),
         ],
         input_output_aliases={0: 0},
-        compiler_params=pltpu.CompilerParams(vmem_limit_bytes=16 * 1024 * 1024),
+        compiler_params=pltpu.CompilerParams(vmem_limit_bytes=56 * 1024 * 1024),
         name="finish",
     )(tile, *halo, total)
 
 
 def shards(object_planes, probe, positions, counts, amplitudes):
     planes, rows, cols = object_planes.shape
-    halo = gather_halo(object_planes)
-    base = jnp.stack([lax.axis_index("ty") * rows - RIM, lax.axis_index("tx") * cols - WIN]).astype(jnp.int32)
-    places = positions[0, 0] - base
-    tile, *outer, part = tile_gradient(counts, places, probe, object_planes, halo, amplitudes[0, 0])
+    places, live, numbers = ordered(positions[0, 0], counts[0, 0], rows, cols)
+    measured = amplitudes[0, 0]
+    *halo, patches, early_part = gather_halo(places, live, probe, object_planes, measured)
+    tile, *outer, part = tile_gradient(places, numbers, probe, object_planes, halo, measured, patches, early_part)
     *outer, total = exchange(outer, part)
     tile, total = finish(tile, outer, total)
     return tile, total.reshape(probe.shape)

time: 146 us -> 135 us (0.925)
  Pallas kernels: 141 us -> 128 us
  other arithmetic: 0.08 us -> 4.89 us
  local copies, waits for them, and re-layouts: 2.97 us -> 0.03 us
    pallas_call x1, Pallas kernels: 93.5 us -> 59.2 us  [exchange(): pl.pallas_call(tail_body, out_shape=(*(jax.ShapeDtypeStruct(h.shape, jnp....]
    pallas_call x1, Pallas kernels: 11.1 us -> 28.8 us  [tile_gradient(): pl.pallas_call(body, out_shape=(jax.ShapeDtypeStruct(tile.shape, f32), *(...]
    unnamed x7 -> x0, local copies, waits for them, and re-layouts: 2.97 us -> none
    reduce_sum x0 -> x3, other arithmetic: none -> 2.38 us  [the longest x1 1.4 us: ordered(): inner = jnp.sum((inside & (slot < count)).astype(jnp.int32))]
    pallas_call x1, Pallas kernels: 32.6 us -> 34.7 us  [gather_halo(): pl.pallas_call(halo_body, out_shape=(*halo_shapes(tile), jax.ShapeDtypeSt...]
    pallas_call x1, Pallas kernels: 4.09 us -> 5.59 us  [finish(): pl.pallas_call(finish_body, out_shape=(jax.ShapeDtypeStruct(tile.shape, j...]
where the time goes in v3:
time: 135 us
  Pallas kernels  128 us (95%)
  other arithmetic  4.89 us (4%)
  between operations  1.99 us (1%)
    pallas_call x1, Pallas kernels, exchange(): pl.pallas_call(tail_body, out_shape=(*(jax.ShapeDtypeStruct(h.shape, jnp....  59.2 us
    pallas_call x1, Pallas kernels, gather_halo(): pl.pallas_call(halo_body, out_shape=(*halo_shapes(tile), jax.ShapeDtypeSt...  34.7 us
    pallas_call x1, Pallas kernels, tile_gradient(): pl.pallas_call(body, out_shape=(jax.ShapeDtypeStruct(tile.shape, f32), *(...  28.8 us
    pallas_call x1, Pallas kernels, finish(): pl.pallas_call(finish_body, out_shape=(jax.ShapeDtypeStruct(tile.shape, j...  5.59 us

profile of v3, /device:TPU:1, one launch (start us, length us, event | category | flops | bytes accessed | tf_op | source)
XLA Modules:
  0.0 135.2 jit_solution(777369306536278542)
XLA Ops:
  1.3 1.4 %fusion.5 = (s32[]{:T(128)}, pred[96,1]{0,1:T(4,128)(4,1)S(1)}, s32[96,1]{0,1:T(1,128)S(1)}) fusion(s32[]{:T(128)} %bitcast.39, s32[]{:T(128)S(6)} %mul.21, s32[96,2]{0,1:T(2,128)} %bitcast.44, s32[]{:T(128)S(6)} %mul.22), kind=kLoop, calls=%fused_computation.19 | loop fusion | flops 1247 | bytes 1264 | tf_op jit(solution)/shard_map/reduce_sum | solution.py:456
  3.3 0.6 pad_add_fusion.number_ref
  4.0 0.2 convert_reduce_fusion
  4.1 1.2 compare_convert_fusion.live_ref
  5.3 0.7 clamp_bitcast_fusion
  6.1 0.8 select_reduce_fusion.place_ref
  6.9 34.7 %gather_halo.1 = (f32[2,512,128]{2,1,0:T(8,128)}, f32[2,512,128]{2,1,0:T(8,128)}, f32[2,64,512]{2,1,0:T(8,128)}, f32[2,64,512]{2,1,0:T(8,128)}, f32[4,2,64,128]{...) custom-call(s32[8,96]{1,0:T(8,128)} %select_reduce_fusion.place_ref, ...), custom_call_target="tpu_custom_call" | custom-call | tf_op jit(solution)/shard_map/gather_halo/pallas_call | solution.py:413
  41.6 28.8 %tile_gradient.1 = (f32[2,1024,512]{2,1,0:T(8,128)}, f32[2,512,128]{2,1,0:T(8,128)}, f32[2,512,128]{2,1,0:T(8,128)}, f32[2,64,512]{2,1,0:T(8,128)}, f32[2,64,512...) custom-call(s32[8,96]{1,0:T(8,128)} %select_reduce_fusion.place_ref, s32[2]{0:T(128)} %pad_add_fusion.number_ref, ...), custom_call_target="tpu_custom_call" | custom-call | tf_op jit(solution)/shard_map/tile_gradient/pallas_call | solution.py:259
  70.3 59.2 %exchange.1 = (f32[2,512,128]{2,1,0:T(8,128)}, f32[2,512,128]{2,1,0:T(8,128)}, f32[2,64,512]{2,1,0:T(8,128)}, f32[2,64,512]{2,1,0:T(8,128)}, f32[4,2,64,128]{3,2,1,0:T(8,128)}, /*index=5*/f32[16,32,128]{2,1,0:T(8,128)}) custom-call(f32[2,512,128]{2,1,0:T(8,128)} %get-tuple-element.32.left_ref, f32[2,512,128]{2,1,0:T(8,128)} %get-tuple-element.33.right_ref, ...), custom_call_target="tpu_custom_call" | custom-call | tf_op jit(solution)/shard_map/exchange/pallas_call | solution.py:576
  129.6 5.6 %finish.1 = (f32[2,1024,512]{2,1,0:T(8,128)}, f32[16,32,128]{2,1,0:T(8,128)}) custom-call(f32[2,1024,512]{2,1,0:T(8,128)} %get-tuple-element.31.tile_ref, f32[2,512,128]{2,1,0:T(8,128)} %get-tuple-element.38.left_ref, f32[2,512,128]{2,1,0:T(8,128)} %get-tuple-element.39.right_ref, ...), custom_call_target="tpu_custom_call", output_to_operand_aliasing={{0}: (0, {})} | custom-call | tf_op jit(solution)/shard_map/finish/pallas_call | solution.py:652
  (8 shorter events, 0.1 us)

commit v4 on v3

--- a/solution.py
+++ b/solution.py
@@ -16,6 +16,7 @@
 SLOTS_ALL = 8 * 16 * 96
 U = 8
 EARLY = 48
+LATE = 16
 
 
 def matrices():
@@ -110,25 +111,50 @@
     return window
 
 
-def put(grad, row, q, shift, values):
+def put(grad, row, q, shift, values, q_next=None):
     here = pl.ds(row, WIN)
     after = lax.broadcasted_iota(jnp.int32, (WIN, WIN), 1) >= shift
+    q_next = q + 1 if q_next is None else q_next
     for plane, value in enumerate(values):
         turned = pltpu.roll(value, shift, 1)
         grad[plane, q, here, :] += jnp.where(after, turned, 0.0)
-        grad[plane, q + 1, here, :] += jnp.where(after, 0.0, turned)
+        grad[plane, q_next, here, :] += jnp.where(after, 0.0, turned)
+
+
+def pack(value, high):
+    half = value.shape[0] // 2
+    first, second = value[:half], value[half:]
+    near = lax.broadcasted_iota(jnp.int32, first.shape, 1) < RIM
+    if high:
+        first = pltpu.roll(first, RIM, 1)
+    else:
+        second = pltpu.roll(second, RIM, 1)
+    return jnp.where(near, first, second)
+
+
+def unpack(packed, high):
+    turned = pltpu.roll(packed, RIM, 1)
+    return (turned, packed) if high else (packed, turned)
+
+
+def deposit(grad, patches, info_of, first, end):
+    for u in range(U):
+        @pl.when(first + u < end)
+        def _(place=first + u):
+            row, q, shift, q_next = info_of(place)
+            put(grad, row, q, shift, (patches[place, 0], patches[place, 1]), q_next)
 
 
 def body(
     place_ref, number_ref, probe_ref, w_ref, tile_ref, left_ref, right_ref, top_ref, bottom_ref, corner_ref,
     measured_ref, patch_ref, part_ref,
     grad_tile, grad_left, grad_right, grad_top, grad_bottom, grad_corner, probe_out,
-    obj, grad, held, sides, patches, in_sems, held_sems, patch_sem,
+    obj, grad, held, sides, corners, patches, in_sems, held_sems, patch_sems,
 ):
     rows = tile_ref.shape[1]
     cols = tile_ref.shape[2]
     tiles = cols // WIN
-    begin, count = number_ref[0], number_ref[1]
+    begin, count, early = number_ref[0], number_ref[1], number_ref[2]
     slots_max = place_ref.shape[1]
 
     def fetch(place):
@@ -149,26 +175,38 @@
         loads.append((tile_ref.at[:, :, span], obj.at[:, q + 1, pl.ds(RIM, rows), :]))
         loads.append((top_ref.at[:, :, span], obj.at[:, q + 1, pl.ds(0, RIM), :]))
         loads.append((bottom_ref.at[:, :, span], obj.at[:, q + 1, pl.ds(low, RIM), :]))
-    for i, (q, start) in enumerate(((0, 0), (last, 0), (0, low), (last, low))):
-        loads.append((corner_ref.at[i], obj.at[:, q, pl.ds(start, RIM), :]))
+    loads.append((corner_ref, corners))
     loads.append((left_ref, sides.at[0]))
     loads.append((right_ref, sides.at[1]))
     loads = [pltpu.make_async_copy(a, b, in_sems.at[i]) for i, (a, b) in enumerate(loads)]
-    early = pltpu.make_async_copy(patch_ref, patches, patch_sem)
-    early.start()
-    for copy in loads:
+    pieces = patch_ref.shape[0] // U
+    chunks = [
+        pltpu.make_async_copy(patch_ref.at[pl.ds(i * U, U)], patches.at[pl.ds(i * U, U)], patch_sems.at[i])
+        for i in range(pieces)
+    ]
+    for copy in chunks[:2] + loads + chunks[2:]:
         copy.start()
     grad[...] = jnp.zeros_like(grad)
     probe_out[...] = part_ref[...]
+
+    def info_of(place):
+        safe = jnp.minimum(place, slots_max - 1)
+        row, col = place_ref[1, safe], place_ref[2, safe]
+        return row, col // WIN, lax.rem(col, WIN), col // WIN + 1
+
+    for i, copy in enumerate(chunks):
+        copy.wait()
+        deposit(grad, patches, info_of, i * U, early)
     for copy in loads:
         copy.wait()
-    first_half = pl.ds(RIM, rows // 2)
-    second_half = pl.ds(middle, rows // 2)
     for plane in range(2):
-        obj[plane, 0, first_half, :] = pltpu.roll(sides[0, plane], RIM, 1)
-        obj[plane, 0, second_half, :] = sides[0, plane]
-        obj[plane, last, first_half, :] = sides[1, plane]
-        obj[plane, last, second_half, :] = pltpu.roll(sides[1, plane], RIM, 1)
+        for q, high in ((0, True), (last, False)):
+            side = 0 if high else 1
+            pieces = ((corners[side, plane], 0), (sides[side, plane], RIM), (corners[2 + side, plane], low))
+            for packed, start in pieces:
+                half = packed.shape[0]
+                for i, value in enumerate(unpack(packed, high)):
+                    obj[plane, q, pl.ds(start + i * half, half), :] = value
     ty, tx = lax.axis_index("ty"), lax.axis_index("tx")
 
     @pl.when(ty == 0)
@@ -187,25 +225,14 @@
     def _():
         obj[:, last] = jnp.zeros((2, rows + WIN, WIN), jnp.float32)
 
-
-    def info_of(place):
-        safe = jnp.minimum(place, slots_max - 1)
-        row, col = place_ref[1, safe], place_ref[2, safe]
-        return row, col // WIN, lax.rem(col, WIN)
-
-    early.wait()
-
-    @pl.loop(0, begin)
-    def _(place):
-        put(grad, *info_of(place), (patches[place, 0], patches[place, 1]))
 
     @pl.loop(0, (count - begin + U - 1) // U)
     def _(group):
         places = [begin + group * U + u for u in range(U)]
         wins = []
         for place in places:
-            row, q, shift = info_of(place)
-            wins.append(take(obj, row, q, q + 1, shift))
+            row, q, shift, q_next = info_of(place)
+            wins.append(take(obj, row, q, q_next, shift))
         for place in places:
             @pl.when(place < count)
             def _():
@@ -214,7 +241,8 @@
         live = [jnp.where(place < count, 1.0, 0.0) for place in places]
         results = inverse(forward(wins, probe_ref, held_now, live, w_ref), wins, probe_ref, w_ref)
         for place, (grad_re, grad_im, terms) in zip(places, results):
-            put(grad, *info_of(place), (grad_re, grad_im))
+            row, q, shift, q_next = info_of(place)
+            put(grad, row, q, shift, (grad_re, grad_im), q_next)
         for i in range(4):
             probe_out[i // 2, i % 2] += sum(r[2][i] for r in results)
         for place in places:
@@ -228,20 +256,19 @@
         stores.append((grad.at[:, q + 1, pl.ds(RIM, rows), :], grad_tile.at[:, :, span]))
         stores.append((grad.at[:, q + 1, pl.ds(0, RIM), :], grad_top.at[:, :, span]))
         stores.append((grad.at[:, q + 1, pl.ds(low, RIM), :], grad_bottom.at[:, :, span]))
-    for i, (q, start) in enumerate(((0, 0), (last, 0), (0, low), (last, low))):
-        stores.append((grad.at[:, q, pl.ds(start, RIM), :], grad_corner.at[i]))
+    stores.append((corners, grad_corner))
     stores.append((sides.at[0], grad_left))
     stores.append((sides.at[1], grad_right))
     stores = [pltpu.make_async_copy(a, b, in_sems.at[i]) for i, (a, b) in enumerate(stores)]
-    for copy in stores[:-2]:
+    for copy in stores[:-3]:
         copy.start()
-    near = lax.broadcasted_iota(jnp.int32, (rows // 2, WIN), 1) < RIM
     for plane in range(2):
-        sides[0, plane] = jnp.where(near, pltpu.roll(grad[plane, 0, first_half, :], RIM, 1), grad[plane, 0, second_half, :])
-        sides[1, plane] = jnp.where(
-            near, grad[plane, last, first_half, :], pltpu.roll(grad[plane, last, second_half, :], RIM, 1)
-        )
-    for copy in stores[-2:]:
+        for q, high in ((0, True), (last, False)):
+            side = 0 if high else 1
+            corners[side, plane] = pack(grad[plane, q, pl.ds(0, RIM), :], high)
+            corners[2 + side, plane] = pack(grad[plane, q, pl.ds(low, RIM), :], high)
+            sides[side, plane] = pack(grad[plane, q, pl.ds(RIM, rows), :], high)
+    for copy in stores[-3:]:
         copy.start()
     for copy in stores:
         copy.wait()
@@ -255,7 +282,7 @@
     vmem = pl.BlockSpec(memory_space=pltpu.VMEM)
     hbm = pl.BlockSpec(memory_space=pl.ANY)
     extent = (planes, tiles + 2, rows + WIN, WIN)
-    copies = 3 * tiles + 6
+    copies = 3 * tiles + 3
     return pl.pallas_call(
         body,
         out_shape=(
@@ -270,10 +297,11 @@
             pltpu.VMEM(extent, f32),
             pltpu.VMEM((AHEAD, WIN, WIN), f32),
             pltpu.VMEM((2, planes, rows // 2, WIN), f32),
+            pltpu.VMEM((4, planes, RIM // 2, WIN), f32),
             pltpu.VMEM(patches.shape, f32),
             pltpu.SemaphoreType.DMA((copies,)),
             pltpu.SemaphoreType.DMA((AHEAD,)),
-            pltpu.SemaphoreType.DMA,
+            pltpu.SemaphoreType.DMA((patches.shape[0] // U,)),
         ],
         compiler_params=pltpu.CompilerParams(vmem_limit_bytes=56 * 1024 * 1024),
         name="tile_gradient",
@@ -298,10 +326,45 @@
         pl.semaphore_signal(barrier, inc=1, device_id=partner, device_id_type=MESH)
 
 
+def inner_patches(
+    begin, place_ref, live_ref, probe_ref, w_ref, obj, held, patches, patch_out, patch_sems, add
+):
+    def store(group):
+        turn = lax.rem(group, 2)
+        return pltpu.make_async_copy(patches.at[turn], patch_out.at[pl.ds(group * U, U)], patch_sems.at[turn])
+
+    groups = patch_out.shape[0] // U
+
+    @pl.loop(0, groups)
+    def _(group):
+        turn = lax.rem(group, 2)
+
+        @pl.when(group >= 2)
+        def _():
+            store(group - 2).wait()
+
+        places = [begin + group * U + u for u in range(U)]
+        wins = [
+            take(obj, place_ref[3, p], place_ref[4, p], place_ref[5, p], place_ref[6, p]) for p in places
+        ]
+        held_now = [held[place_ref[0, p]] for p in places]
+        live = [live_ref[p] for p in places]
+        results = inverse(forward(wins, probe_ref, held_now, live, w_ref), wins, probe_ref, w_ref)
+        for u, (grad_re, grad_im, terms) in enumerate(results):
+            patches[turn, u, 0] = grad_re
+            patches[turn, u, 1] = grad_im
+        for i in range(4):
+            add(i, sum(r[2][i] for r in results))
+        store(group).start()
+
+    for group in range(max(groups - 2, 0), groups):
+        store(group).wait()
+
+
 def halo_body(
     place_ref, live_ref, probe_ref, w_ref, tile_ref, measured_ref,
     left_out, right_out, top_out, bottom_out, corner_out, patch_out, part_out,
-    obj, held, packed, patches, in_sems, held_sem, send_sems, recv_sems, patch_sems,
+    obj, held, packed, corners, patches, in_sems, held_sem, send_sems, recv_sems, patch_sems,
 ):
     rows, cols = tile_ref.shape[1:]
     tiles = cols // WIN
@@ -315,65 +378,33 @@
     measures = pltpu.make_async_copy(measured_ref, held, held_sem)
     measures.start()
     part_out[...] = jnp.zeros_like(part_out)
-    half = rows // 2
-    first, second = pl.ds(0, half), pl.ds(half, half)
-    near = lax.broadcasted_iota(jnp.int32, (half, WIN), 1) < RIM
-    loads[0].wait()
-    for plane in range(2):
-        packed[0, plane] = jnp.where(near, obj[plane, 0, first, :], pltpu.roll(obj[plane, 0, second, :], RIM, 1))
-    loads[tiles - 1].wait()
-    for plane in range(2):
-        packed[1, plane] = jnp.where(
-            near, pltpu.roll(obj[plane, tiles - 1, first, :], RIM, 1), obj[plane, tiles - 1, second, :]
-        )
+    above, below = pl.ds(0, RIM), pl.ds(rows - RIM, RIM)
+    for side, q in enumerate((0, tiles - 1)):
+        loads[q].wait()
+        for plane in range(2):
+            packed[side, plane] = pack(obj[plane, q], side == 1)
+            corners[side, plane] = pack(obj[plane, q, above, :], side == 1)
+            corners[2 + side, plane] = pack(obj[plane, q, below, :], side == 1)
     pl.semaphore_wait(pltpu.get_barrier_semaphore(), len(AROUND))
-    above, below = pl.ds(0, RIM), pl.ds(rows - RIM, RIM)
-    start, stop = pl.ds(0, WIN), pl.ds(cols - WIN, WIN)
     moves = (
         (packed.at[0], right_out, (0, -1)),
         (packed.at[1], left_out, (0, 1)),
         (tile_ref.at[:, above, :], bottom_out, (-1, 0)),
         (tile_ref.at[:, below, :], top_out, (1, 0)),
-        (tile_ref.at[:, below, stop], corner_out.at[0], (1, 1)),
-        (tile_ref.at[:, below, start], corner_out.at[1], (1, -1)),
-        (tile_ref.at[:, above, stop], corner_out.at[2], (-1, 1)),
-        (tile_ref.at[:, above, start], corner_out.at[3], (-1, -1)),
+        (corners.at[3], corner_out.at[0], (1, 1)),
+        (corners.at[2], corner_out.at[1], (1, -1)),
+        (corners.at[1], corner_out.at[2], (-1, 1)),
+        (corners.at[0], corner_out.at[3], (-1, -1)),
     )
     halo = send(moves, send_sems, recv_sems, wait=False)
     for q in range(1, tiles - 1):
         loads[q].wait()
     measures.wait()
 
-    def store(group):
-        turn = lax.rem(group, 2)
-        return pltpu.make_async_copy(patches.at[turn], patch_out.at[pl.ds(group * U, U)], patch_sems.at[turn])
-
-    groups = patch_out.shape[0] // U
-
-    @pl.loop(0, groups)
-    def _(group):
-        turn = lax.rem(group, 2)
-
-        @pl.when(group >= 2)
-        def _():
-            store(group - 2).wait()
-
-        places = [group * U + u for u in range(U)]
-        wins = [
-            take(obj, place_ref[3, p], place_ref[4, p], place_ref[5, p], place_ref[6, p]) for p in places
-        ]
-        held_now = [held[place_ref[0, p]] for p in places]
-        live = [live_ref[p] for p in places]
-        results = inverse(forward(wins, probe_ref, held_now, live, w_ref), wins, probe_ref, w_ref)
-        for u, (grad_re, grad_im, terms) in enumerate(results):
-            patches[turn, u, 0] = grad_re
-            patches[turn, u, 1] = grad_im
-        for i in range(4):
-            part_out[i // 2, i % 2] += sum(r[2][i] for r in results)
-        store(group).start()
-
-    for group in range(max(groups - 2, 0), groups):
-        store(group).wait()
+    def add(i, term):
+        part_out[i // 2, i % 2] += term
+
+    inner_patches(0, place_ref, live_ref, probe_ref, w_ref, obj, held, patches, patch_out, patch_sems, add)
     for copy in halo:
         copy.wait()
 
@@ -400,7 +431,7 @@
 
 def halo_shapes(tile):
     planes, rows, cols = tile.shape
-    shapes = [(planes, rows // 2, WIN)] * 2 + [(planes, RIM, cols)] * 2 + [(4, planes, RIM, WIN)]
+    shapes = [(planes, rows // 2, WIN)] * 2 + [(planes, RIM, cols)] * 2 + [(4, planes, RIM // 2, WIN)]
     return tuple(jax.ShapeDtypeStruct(s, jnp.float32) for s in shapes)
 
 
@@ -423,6 +454,7 @@
             pltpu.VMEM((planes, cols // WIN, rows, WIN), f32),
             pltpu.VMEM(measured.shape, f32),
             pltpu.VMEM((2, planes, rows // 2, WIN), f32),
+            pltpu.VMEM((4, planes, RIM // 2, WIN), f32),
             pltpu.VMEM((2, U, planes, WIN, WIN), f32),
             pltpu.SemaphoreType.DMA((cols // WIN,)),
             pltpu.SemaphoreType.DMA,
@@ -455,13 +487,17 @@
     table = jnp.sum(jnp.where(hit[None], table[:, None, :], 0), axis=2)
     inner = jnp.sum((inside & (slot < count)).astype(jnp.int32))
     live = (slot < inner).astype(jnp.float32)
-    return table, live, jnp.stack([jnp.minimum(inner, EARLY), count])
+    early = jnp.minimum(inner, EARLY)
+    done = jnp.minimum(inner, EARLY + LATE)
+    return table, live, jnp.stack([done, count, early, done - early])
 
 
 def tail_body(
-    left_ref, right_ref, top_ref, bottom_ref, corner_ref, part_ref,
-    left_out, right_out, top_out, bottom_out, corner_out, total_out,
-    gathered, stage, send_sems, recv_sems, tx_send, tx_recv, ty_send, ty_recv, out_send, out_recv,
+    place_ref, live_ref, probe_ref, w_ref, tile_ref, measured_ref,
+    left_ref, right_ref, top_ref, bottom_ref, corner_ref, start_ref,
+    left_out, right_out, top_out, bottom_out, corner_out, patch_out, total_out,
+    obj, held, patches, part_ref, gathered, stage, in_sems, held_sem, patch_sems,
+    send_sems, recv_sems, tx_send, tx_recv, ty_send, ty_recv, out_send, out_recv,
 ):
     ty, tx = lax.axis_index("ty"), lax.axis_index("tx")
     ny, nx = lax.axis_size("ty"), lax.axis_size("tx")
@@ -477,6 +513,15 @@
     def _(k):
         pl.semaphore_signal(barrier, inc=1, device_id={"ty": lax.rem(ty + k, ny)}, device_id_type=MESH)
 
+    tiles = tile_ref.shape[2] // WIN
+    loads = [
+        pltpu.make_async_copy(tile_ref.at[:, :, pl.ds(q * WIN, WIN)], obj.at[:, q], in_sems.at[q])
+        for q in range(tiles)
+    ]
+    loads.append(pltpu.make_async_copy(measured_ref, held, held_sem))
+    for copy in loads:
+        copy.start()
+    part_ref[...] = start_ref[...]
     pl.semaphore_wait(barrier, len(diagonal) + nx - 1 + ny - 1)
 
     def to_column(k, source, target, sends, receives):
@@ -507,10 +552,6 @@
 
     def share(k):
         return to_column(k, total_out.at[tx], total_out.at[tx], out_send, out_recv)
-
-    @pl.loop(1, nx)
-    def _(k):
-        spread(k).start()
 
     moves = (
         (left_ref, right_out, (0, -1)),
@@ -523,6 +564,18 @@
         (corner_ref.at[3], corner_out.at[0], (1, 1)),
     )
     halo = send(moves, send_sems, recv_sems, wait=False)
+    for copy in loads:
+        copy.wait()
+
+    def add(i, term):
+        each = part_ref.shape[0] // 4
+        part_ref[pl.ds(i * each, each)] += term.reshape(each, WIN // each, WIN)
+
+    inner_patches(EARLY, place_ref, live_ref, probe_ref, w_ref, obj, held, patches, patch_out, patch_sems, add)
+
+    @pl.loop(1, nx)
+    def _(k):
+        spread(k).start()
 
     stage[ty] = part_ref[tx]
 
@@ -568,22 +621,32 @@
         to_row(k).wait_send()
 
 
-def exchange(halo, part):
+def exchange(places, live, probe, tile, measured, halo, part):
     hbm = pl.BlockSpec(memory_space=pl.ANY)
     vmem = pl.BlockSpec(memory_space=pltpu.VMEM)
+    smem = pl.BlockSpec(memory_space=pltpu.SMEM)
+    planes, rows, cols = tile.shape
     ny, nx = lax.axis_size("ty"), lax.axis_size("tx")
     chunk = (part.size // (nx * WIN), WIN)
     return pl.pallas_call(
         tail_body,
         out_shape=(
             *(jax.ShapeDtypeStruct(h.shape, jnp.float32) for h in halo),
+            jax.ShapeDtypeStruct((LATE, planes, WIN, WIN), jnp.float32),
             jax.ShapeDtypeStruct((nx, *chunk), jnp.float32),
         ),
-        in_specs=[hbm] * 5 + [vmem],
-        out_specs=(*[hbm] * 5, vmem),
+        in_specs=[smem, smem, vmem, vmem] + [hbm] * 7 + [vmem],
+        out_specs=(*[hbm] * 6, vmem),
         scratch_shapes=[
+            pltpu.VMEM((planes, cols // WIN, rows, WIN), jnp.float32),
+            pltpu.VMEM(measured.shape, jnp.float32),
+            pltpu.VMEM((2, U, planes, WIN, WIN), jnp.float32),
+            pltpu.VMEM((nx, *chunk), jnp.float32),
             pltpu.VMEM((nx, *chunk), jnp.float32),
             pltpu.VMEM((ny, *chunk), jnp.float32),
+            pltpu.SemaphoreType.DMA((cols // WIN,)),
+            pltpu.SemaphoreType.DMA,
+            pltpu.SemaphoreType.DMA((2,)),
             pltpu.SemaphoreType.DMA((8,)),
             pltpu.SemaphoreType.DMA((8,)),
             pltpu.SemaphoreType.DMA((nx,)),
@@ -597,72 +660,99 @@
             collective_id=1, has_side_effects=True, vmem_limit_bytes=56 * 1024 * 1024
         ),
         name="exchange",
-    )(*halo, part.reshape(nx, *chunk))
+    )(places, live, probe, jnp.asarray(matrices()), tile, measured, *halo, part.reshape(nx, *chunk))
 
 
 def finish_body(
-    tile_ref, left_ref, right_ref, top_ref, bottom_ref, corner_ref, total_ref, out_ref, total_out, edge, strip, in_sems
+    place_ref, number_ref, tile_ref, left_ref, right_ref, top_ref, bottom_ref, corner_ref, patch_ref, total_ref,
+    out_ref, total_out, grad, sides, rims, corners, patches, in_sems, more_sems,
 ):
     planes, rows, cols = tile_ref.shape
+    tiles = cols // WIN
     ty, tx = lax.axis_index("ty"), lax.axis_index("tx")
     ny, nx = lax.axis_size("ty"), lax.axis_size("tx")
-    half = rows // 2
-    ends = (pl.ds(0, RIM), pl.ds(rows - RIM, RIM))
-    sides = (pl.ds(0, WIN), pl.ds(cols - WIN, WIN))
-    inner = pl.ds(WIN, cols - 2 * WIN)
-    parts = [(out_ref.at[:, :, span], edge.at[i]) for i, span in enumerate(sides)]
-    parts += [(out_ref.at[:, span, inner], strip.at[i]) for i, span in enumerate(ends)]
-    reads = [pltpu.make_async_copy(a, b, in_sems.at[i]) for i, (a, b) in enumerate(parts)]
-    for copy in reads:
+    late = number_ref[3]
+    spans = [pl.ds(q * WIN, WIN) for q in range(tiles)]
+    more = (
+        (patch_ref, patches),
+        (left_ref, sides.at[0]),
+        (right_ref, sides.at[1]),
+        (top_ref, rims.at[0]),
+        (bottom_ref, rims.at[1]),
+        (corner_ref, corners),
+    )
+    more = [pltpu.make_async_copy(a, b, more_sems.at[i]) for i, (a, b) in enumerate(more)]
+    reads = [
+        pltpu.make_async_copy(tile_ref.at[:, :, span], grad.at[:, q], in_sems.at[q]) for q, span in enumerate(spans)
+    ]
+    for copy in reads + more:
         copy.start()
     total_out[...] = total_ref[...]
-    lane = lax.broadcasted_iota(jnp.int32, (half, WIN), 1)
-    near = lane < RIM
-    lane = lane[:RIM]
     no_side = (tx == 0, tx == nx - 1)
     no_end = (ty == 0, ty == ny - 1)
-    for copy in reads:
+    ends = (0, rows - RIM)
+    for copy in reads + more:
         copy.wait()
+
+    def info_of(place):
+        at = EARLY + place
+        return place_ref[3, at], place_ref[4, at], place_ref[6, at], place_ref[5, at]
+
+    for first in range(0, patches.shape[0], U):
+        deposit(grad, patches, info_of, first, late)
+
+    def side_add(plane, side, start, packed, gone):
+        high = side == 1
+        half = packed.shape[0]
+        far = lax.broadcasted_iota(jnp.int32, packed.shape, 1) >= RIM
+        mine = far if high else jnp.logical_not(far)
+        for i, value in enumerate(unpack(packed, high)):
+            here = pl.ds(start + i * half, half)
+            value = jnp.where(gone, 0.0, value)
+            grad[plane, side * (tiles - 1), here, :] += jnp.where(mine, value, 0.0)
+
     for plane in range(2):
-        for i, packed in enumerate((left_ref, right_ref)):
-            value = jnp.where(no_side[i], 0.0, packed[plane])
-            turned = pltpu.roll(value, RIM, 1)
-            mine = near if i == 0 else jnp.logical_not(near)
-            first, second = (value, turned) if i == 0 else (turned, value)
-            edge[i, plane, pl.ds(0, half), :] += jnp.where(mine, first, 0.0)
-            edge[i, plane, pl.ds(half, half), :] += jnp.where(mine, second, 0.0)
-        for j, rim in enumerate((top_ref, bottom_ref)):
-            for i in range(2):
-                value = jnp.where(no_end[j], 0.0, rim[plane, :, sides[i]])
-                gone = jnp.logical_or(no_side[i], no_end[j])
-                value += jnp.where(gone, 0.0, corner_ref[2 * j + i, plane])
-                edge[i, plane, ends[j], :] += value
-            strip[j, plane] += jnp.where(no_end[j], 0.0, rim[plane, :, inner])
-    writes = [pltpu.make_async_copy(b, a, in_sems.at[i]) for i, (a, b) in enumerate(parts)]
+        for side in range(2):
+            side_add(plane, side, 0, sides[side, plane], no_side[side])
+            for end in range(2):
+                gone = jnp.logical_or(no_side[side], no_end[end])
+                side_add(plane, side, ends[end], corners[2 * end + side, plane], gone)
+        for end in range(2):
+            for q in range(tiles):
+                value = jnp.where(no_end[end], 0.0, rims[end, plane, :, spans[q]])
+                grad[plane, q, pl.ds(ends[end], RIM), :] += value
+    writes = [
+        pltpu.make_async_copy(grad.at[:, q], out_ref.at[:, :, span], in_sems.at[q]) for q, span in enumerate(spans)
+    ]
     for copy in writes:
         copy.start()
     for copy in writes:
         copy.wait()
 
 
-def finish(tile, halo, total):
+def finish(places, numbers, tile, halo, patches, total):
     planes, rows, cols = tile.shape
     hbm = pl.BlockSpec(memory_space=pl.ANY)
     vmem = pl.BlockSpec(memory_space=pltpu.VMEM)
+    smem = pl.BlockSpec(memory_space=pltpu.SMEM)
+    f32 = jnp.float32
     return pl.pallas_call(
         finish_body,
-        out_shape=(jax.ShapeDtypeStruct(tile.shape, jnp.float32), jax.ShapeDtypeStruct(total.shape, jnp.float32)),
-        in_specs=[hbm] + [vmem] * 6,
+        out_shape=(jax.ShapeDtypeStruct(tile.shape, f32), jax.ShapeDtypeStruct(total.shape, f32)),
+        in_specs=[smem, smem] + [hbm] * 7 + [vmem],
         out_specs=(hbm, vmem),
         scratch_shapes=[
-            pltpu.VMEM((2, planes, rows, WIN), jnp.float32),
-            pltpu.VMEM((2, planes, RIM, cols - 2 * WIN), jnp.float32),
-            pltpu.SemaphoreType.DMA((4,)),
+            pltpu.VMEM((planes, cols // WIN, rows, WIN), f32),
+            pltpu.VMEM((2, planes, rows // 2, WIN), f32),
+            pltpu.VMEM((2, planes, RIM, cols), f32),
+            pltpu.VMEM((4, planes, RIM // 2, WIN), f32),
+            pltpu.VMEM(patches.shape, f32),
+            pltpu.SemaphoreType.DMA((cols // WIN,)),
+            pltpu.SemaphoreType.DMA((6,)),
         ],
-        input_output_aliases={0: 0},
         compiler_params=pltpu.CompilerParams(vmem_limit_bytes=56 * 1024 * 1024),
         name="finish",
-    )(tile, *halo, total)
+    )(places, numbers, tile, *halo, patches, total)
 
 
 def shards(object_planes, probe, positions, counts, amplitudes):
@@ -671,8 +761,8 @@
     measured = amplitudes[0, 0]
     *halo, patches, early_part = gather_halo(places, live, probe, object_planes, measured)
     tile, *outer, part = tile_gradient(places, numbers, probe, object_planes, halo, measured, patches, early_part)
-    *outer, total = exchange(outer, part)
-    tile, total = finish(tile, outer, total)
+    *outer, patches, total = exchange(places, live, probe, object_planes, measured, outer, part)
+    tile, total = finish(places, numbers, tile, outer, patches, total)
     return tile, total.reshape(probe.shape)
 
 

time: 135 us -> 129 us (0.956)
  Pallas kernels: 128 us -> 121 us
    pallas_call x1, Pallas kernels: 59.2 us -> 50.5 us  [exchange(): pl.pallas_call(tail_body, out_shape=(*(jax.ShapeDtypeStruct(h.shape, jnp....]
    pallas_call x1, Pallas kernels: 5.59 us -> 7.42 us  [finish(): pl.pallas_call(finish_body, out_shape=(jax.ShapeDtypeStruct(tile.shape, f...]
where the time goes in v4:
time: 129 us
  Pallas kernels  121 us (94%)
  other arithmetic  4.85 us (4%)
  between operations  2.8 us (2%)
    pallas_call x1, Pallas kernels, exchange(): pl.pallas_call(tail_body, out_shape=(*(jax.ShapeDtypeStruct(h.shape, jnp....  50.5 us
    pallas_call x1, Pallas kernels, gather_halo(): pl.pallas_call(halo_body, out_shape=(*halo_shapes(tile), jax.ShapeDtypeSt...  33.6 us
    pallas_call x1, Pallas kernels, tile_gradient(): pl.pallas_call(body, out_shape=(jax.ShapeDtypeStruct(tile.shape, f32), *(...  29.8 us
    pallas_call x1, Pallas kernels, finish(): pl.pallas_call(finish_body, out_shape=(jax.ShapeDtypeStruct(tile.shape, f...  7.42 us

profile of v4, /device:TPU:1, one launch (start us, length us, event | category | flops | bytes accessed | tf_op | source)
XLA Modules:
  0.0 129.1 jit_solution(3039535178784692059)
XLA Ops:
  1.3 1.4 %fusion.5 = (s32[]{:T(128)}, pred[96,1]{0,1:T(4,128)(4,1)S(1)}, s32[96,1]{0,1:T(1,128)S(1)}) fusion(s32[]{:T(128)} %bitcast.41, s32[]{:T(128)S(6)} %mul.21, s32[96,2]{0,1:T(2,128)} %bitcast.47, s32[]{:T(128)S(6)} %mul.22), kind=kLoop, calls=%fused_computation.19 | loop fusion | flops 1247 | bytes 1264 | tf_op jit(solution)/shard_map/reduce_sum | solution.py:488
  4.0 0.6 pad_add_fusion.number_ref
  4.6 1.2 compare_convert_fusion.live_ref
  5.7 0.2 convert_reduce_fusion
  5.9 0.7 clamp_bitcast_fusion
  6.7 0.8 select_reduce_fusion.place_ref
  7.5 33.6 %gather_halo.1 = (f32[2,512,128]{2,1,0:T(8,128)}, f32[2,512,128]{2,1,0:T(8,128)}, f32[2,64,512]{2,1,0:T(8,128)}, f32[2,64,512]{2,1,0:T(8,128)}, f32[4,2,32,128]{...) custom-call(s32[8,96]{1,0:T(8,128)} %select_reduce_fusion.place_ref, ...), custom_call_target="tpu_custom_call" | custom-call | tf_op jit(solution)/shard_map/gather_halo/pallas_call | solution.py:444
  41.1 29.8 %tile_gradient.1 = (f32[2,1024,512]{2,1,0:T(8,128)}, f32[2,512,128]{2,1,0:T(8,128)}, f32[2,512,128]{2,1,0:T(8,128)}, f32[2,64,512]{2,1,0:T(8,128)}, f32[2,64,512...) custom-call(s32[8,96]{1,0:T(8,128)} %select_reduce_fusion.place_ref, s32[4]{0:T(128)} %pad_add_fusion.number_ref, ...), custom_call_target="tpu_custom_call" | custom-call | tf_op jit(solution)/shard_map/tile_gradient/pallas_call | solution.py:286
  70.9 50.5 %exchange.1 = (f32[2,512,128]{2,1,0:T(8,128)}, f32[2,512,128]{2,1,0:T(8,128)}, f32[2,64,512]{2,1,0:T(8,128)}, f32[2,64,512]{2,1,0:T(8,128)}, f32[4,2,32,128]{3,2...) custom-call(s32[8,96]{1,0:T(8,128)} %select_reduce_fusion.place_ref, f32[96]{0:T(128)} %compare_convert_fusion.live_ref, ...), custom_call_target="tpu_custom_call" | custom-call | tf_op jit(solution)/shard_map/exchange/pallas_call | solution.py:631
  121.5 7.4 %finish.1 = (f32[2,1024,512]{2,1,0:T(8,128)}, f32[16,32,128]{2,1,0:T(8,128)}) custom-call(s32[8,96]{1,0:T(8,128)} %select_reduce_fusion.place_ref, s32[4]{0:T(128)} %pad_add_fusion.number_ref, f32[2,1024,512]{2,1,0:T(8,128)} %get-tuple-element.32.tile_ref, f32[2,512,128]{2,1,0:T(8,128)} %get-tuple-element.39.left_ref, ...), custom_call_target="tpu_custom_call" | custom-call | tf_op jit(solution)/shard_map/finish/pallas_call | solution.py:739
  (8 shorter events, 0.1 us)

commit v5 on v4

--- a/solution.py
+++ b/solution.py
@@ -15,6 +15,9 @@
 MESH = pl.DeviceIdType.MESH
 SLOTS_ALL = 8 * 16 * 96
 U = 8
+SMALL = 4
+WIDE = 16
+STAGES = 7
 EARLY = 48
 LATE = 16
 
@@ -62,42 +65,49 @@
     return dot(w_ref[k, 0], high) + dot(w_ref[k, 0], low) + dot(w_ref[k, 1], high)
 
 
-def forward(wins, probe_ref, measured, live, w_ref):
+def slot_steps(window, probe_ref, measured, live, w_ref):
+    a, b = window
     p0r, p0i = probe_ref[0, 0], probe_ref[0, 1]
     p1r, p1i = probe_ref[1, 0], probe_ref[1, 1]
-    waves = [assemble(
+    wave = assemble(
         p0r * a - p0i * b,
         p0r * b + p0i * a,
         p1r * a - p1i * b,
         p1r * b + p1i * a,
-    ) for a, b in wins]
-    xs = []
-    for half in [right_product(v, w_ref, 0) for v in waves]:
-        m0r, m0i, m1r, m1i = blocks(half)
-        xs.append(assemble(m0r, m1r, m0i, m1i))
-    out = []
-    for k, far in enumerate([left_product(v, w_ref, 1) for v in xs]):
-        f0r, f1r, f0i, f1i = blocks(far)
-        intensity = f0r * f0r + f0i * f0i + (f1r * f1r + f1i * f1i)
-        weight = live[k] - (live[k] * measured[k]) * lax.rsqrt(jnp.maximum(intensity, FLOOR))
-        out.append(assemble(weight * f0r, weight * f1r, weight * f0i, weight * f1i))
-    return out
-
-
-def inverse(values, wins, probe_ref, w_ref):
-    p0r, p0i = probe_ref[0, 0], probe_ref[0, 1]
-    p1r, p1i = probe_ref[1, 0], probe_ref[1, 1]
-    xs = []
-    for half in [left_product(v, w_ref, 0) for v in values]:
-        m0r, m1r, m0i, m1i = blocks(half)
-        xs.append(assemble(m0r, m0i, m1r, m1i))
-    out = []
-    for (a, b), back in zip(wins, [right_product(v, w_ref, 1) for v in xs]):
-        b0r, b0i, b1r, b1i = blocks(back)
-        grad_re = p0r * b0r + p0i * b0i + (p1r * b1r + p1i * b1i)
-        grad_im = p0r * b0i - p0i * b0r + (p1r * b1i - p1i * b1r)
-        out.append((grad_re, grad_im, (a * b0r + b * b0i, a * b0i - b * b0r, a * b1r + b * b1i, a * b1i - b * b1r)))
-    return out
+    )
+    yield
+    half = right_product(wave, w_ref, 0)
+    yield
+    m0r, m0i, m1r, m1i = blocks(half)
+    far = left_product(assemble(m0r, m1r, m0i, m1i), w_ref, 1)
+    yield
+    f0r, f1r, f0i, f1i = blocks(far)
+    intensity = f0r * f0r + f0i * f0i + (f1r * f1r + f1i * f1i)
+    weight = live - (live * measured) * lax.rsqrt(jnp.maximum(intensity, FLOOR))
+    value = assemble(weight * f0r, weight * f1r, weight * f0i, weight * f1i)
+    yield
+    half = left_product(value, w_ref, 0)
+    yield
+    m0r, m1r, m0i, m1i = blocks(half)
+    back = right_product(assemble(m0r, m0i, m1r, m1i), w_ref, 1)
+    yield
+    b0r, b0i, b1r, b1i = blocks(back)
+    grad_re = p0r * b0r + p0i * b0i + (p1r * b1r + p1i * b1i)
+    grad_im = p0r * b0i - p0i * b0r + (p1r * b1i - p1i * b1r)
+    yield grad_re, grad_im, (a * b0r + b * b0i, a * b0i - b * b0r, a * b1r + b * b1i, a * b1i - b * b1r)
+
+
+def pipelined(start, finish, size):
+    runs = [None] * size
+    for moment in range(STAGES + size - 1):
+        for u in reversed(range(size)):
+            stage = moment - u
+            if 0 <= stage < STAGES:
+                if stage == 0:
+                    runs[u] = start(u)
+                result = next(runs[u])
+                if stage == STAGES - 1:
+                    finish(u, *result)
 
 
 def take(obj, row, q, q_next, shift):
@@ -226,29 +236,43 @@
         obj[:, last] = jnp.zeros((2, rows + WIN, WIN), jnp.float32)
 
 
-    @pl.loop(0, (count - begin + U - 1) // U)
-    def _(group):
-        places = [begin + group * U + u for u in range(U)]
-        wins = []
-        for place in places:
-            row, q, shift, q_next = info_of(place)
-            wins.append(take(obj, row, q, q_next, shift))
+    def run(first, size):
+        places = [first + u for u in range(size)]
         for place in places:
             @pl.when(place < count)
-            def _():
+            def _(place=place):
                 fetch(place).wait()
-        held_now = [held[lax.rem(place - begin, AHEAD)] for place in places]
-        live = [jnp.where(place < count, 1.0, 0.0) for place in places]
-        results = inverse(forward(wins, probe_ref, held_now, live, w_ref), wins, probe_ref, w_ref)
-        for place, (grad_re, grad_im, terms) in zip(places, results):
-            row, q, shift, q_next = info_of(place)
+        terms = []
+
+        def start(u):
+            row, q, shift, q_next = info_of(places[u])
+            window = take(obj, row, q, q_next, shift)
+            live = jnp.where(places[u] < count, 1.0, 0.0)
+            return slot_steps(window, probe_ref, held[lax.rem(places[u] - begin, AHEAD)], live, w_ref)
+
+        def finish(u, grad_re, grad_im, term):
+            row, q, shift, q_next = info_of(places[u])
             put(grad, row, q, shift, (grad_re, grad_im), q_next)
+            terms.append(term)
+
+        pipelined(start, finish, size)
         for i in range(4):
-            probe_out[i // 2, i % 2] += sum(r[2][i] for r in results)
+            probe_out[i // 2, i % 2] += sum(term[i] for term in terms)
         for place in places:
             @pl.when(place + AHEAD < count)
-            def _():
+            def _(place=place):
                 fetch(place + AHEAD).start()
+
+    rest = count - begin
+    whole = (rest + SMALL - 1) // U
+
+    @pl.loop(0, whole)
+    def _(group):
+        run(begin + group * U, U)
+
+    @pl.when(rest > whole * U)
+    def _():
+        run(begin + whole * U, SMALL)
 
     stores = []
     for q in range(tiles):
@@ -329,11 +353,13 @@
 def inner_patches(
     begin, place_ref, live_ref, probe_ref, w_ref, obj, held, patches, patch_out, patch_sems, add
 ):
+    size = patches.shape[1]
+
     def store(group):
         turn = lax.rem(group, 2)
-        return pltpu.make_async_copy(patches.at[turn], patch_out.at[pl.ds(group * U, U)], patch_sems.at[turn])
-
-    groups = patch_out.shape[0] // U
+        return pltpu.make_async_copy(patches.at[turn], patch_out.at[pl.ds(group * size, size)], patch_sems.at[turn])
+
+    groups = patch_out.shape[0] // size
 
     @pl.loop(0, groups)
     def _(group):
@@ -343,18 +369,20 @@
         def _():
             store(group - 2).wait()
 
-        places = [begin + group * U + u for u in range(U)]
-        wins = [
-            take(obj, place_ref[3, p], place_ref[4, p], place_ref[5, p], place_ref[6, p]) for p in places
-        ]
-        held_now = [held[place_ref[0, p]] for p in places]
-        live = [live_ref[p] for p in places]
-        results = inverse(forward(wins, probe_ref, held_now, live, w_ref), wins, probe_ref, w_ref)
-        for u, (grad_re, grad_im, terms) in enumerate(results):
+        places = [begin + group * size + u for u in range(size)]
+
+        def start(u):
+            p = places[u]
+            window = take(obj, place_ref[3, p], place_ref[4, p], place_ref[5, p], place_ref[6, p])
+            return slot_steps(window, probe_ref, held[place_ref[0, p]], live_ref[p], w_ref)
+
+        def finish(u, grad_re, grad_im, terms):
             patches[turn, u, 0] = grad_re
             patches[turn, u, 1] = grad_im
-        for i in range(4):
-            add(i, sum(r[2][i] for r in results))
+            for i, term in enumerate(terms):
+                add(i, term)
+
+        pipelined(start, finish, size)
         store(group).start()
 
     for group in range(max(groups - 2, 0), groups):
@@ -396,7 +424,7 @@
         (corners.at[1], corner_out.at[2], (-1, 1)),
         (corners.at[0], corner_out.at[3], (-1, -1)),
     )
-    halo = send(moves, send_sems, recv_sems, wait=False)
+    halo = send(moves, send_sems, recv_sems)
     for q in range(1, tiles - 1):
         loads[q].wait()
     measures.wait()
@@ -409,7 +437,7 @@
         copy.wait()
 
 
-def send(moves, send_sems, recv_sems, wait=True):
+def send(moves, send_sems, recv_sems, begin=True):
     copies = [
         pltpu.make_async_remote_copy(
             src_ref=source,
@@ -421,11 +449,9 @@
         )
         for i, (source, target, step) in enumerate(moves)
     ]
-    for copy in copies:
-        copy.start()
-    if wait:
+    if begin:
         for copy in copies:
-            copy.wait()
+            copy.start()
     return copies
 
 
@@ -455,7 +481,7 @@
             pltpu.VMEM(measured.shape, f32),
             pltpu.VMEM((2, planes, rows // 2, WIN), f32),
             pltpu.VMEM((4, planes, RIM // 2, WIN), f32),
-            pltpu.VMEM((2, U, planes, WIN, WIN), f32),
+            pltpu.VMEM((2, WIDE, planes, WIN, WIN), f32),
             pltpu.SemaphoreType.DMA((cols // WIN,)),
             pltpu.SemaphoreType.DMA,
             pltpu.SemaphoreType.DMA((8,)),
@@ -563,7 +589,9 @@
         (corner_ref.at[2], corner_out.at[1], (1, -1)),
         (corner_ref.at[3], corner_out.at[0], (1, 1)),
     )
-    halo = send(moves, send_sems, recv_sems, wait=False)
+    halo = send(moves, send_sems, recv_sems, begin=False)
+    for copy in halo[:2]:
+        copy.start()
     for copy in loads:
         copy.wait()
 
@@ -577,6 +605,8 @@
     def _(k):
         spread(k).start()
 
+    for copy in (halo[2], *halo[4:6]):
+        copy.start()
     stage[ty] = part_ref[tx]
 
     @pl.loop(1, nx)
@@ -588,6 +618,9 @@
     @pl.loop(1, ny)
     def _(k):
         to_row(k).start()
+
+    for copy in (halo[3], *halo[6:]):
+        copy.start()
 
     @pl.loop(1, ny)
     def _(k):
@@ -640,7 +673,7 @@
         scratch_shapes=[
             pltpu.VMEM((planes, cols // WIN, rows, WIN), jnp.float32),
             pltpu.VMEM(measured.shape, jnp.float32),
-            pltpu.VMEM((2, U, planes, WIN, WIN), jnp.float32),
+            pltpu.VMEM((2, WIDE, planes, WIN, WIN), jnp.float32),
             pltpu.VMEM((nx, *chunk), jnp.float32),
             pltpu.VMEM((nx, *chunk), jnp.float32),
             pltpu.VMEM((ny, *chunk), jnp.float32),
@@ -691,7 +724,7 @@
     no_side = (tx == 0, tx == nx - 1)
     no_end = (ty == 0, ty == ny - 1)
     ends = (0, rows - RIM)
-    for copy in reads + more:
+    for copy in (*reads, more[0]):
         copy.wait()
 
     def info_of(place):
@@ -700,6 +733,9 @@
 
     for first in range(0, patches.shape[0], U):
         deposit(grad, patches, info_of, first, late)
+
+    for copy in more[1:]:
+        copy.wait()
 
     def side_add(plane, side, start, packed, gone):
         high = side == 1

time: 129 us -> 120 us (0.930)
  Pallas kernels: 121 us -> 112 us
    pallas_call x1, Pallas kernels: 29.8 us -> 17.6 us  [tile_gradient(): pl.pallas_call(body, out_shape=(jax.ShapeDtypeStruct(tile.shape, f32), *(...]
    pallas_call x1, Pallas kernels: 50.5 us -> 53.7 us  [exchange(): pl.pallas_call(tail_body, out_shape=(*(jax.ShapeDtypeStruct(h.shape, jnp....]
where the time goes in v5:
time: 120 us
  Pallas kernels  112 us (93%)
  other arithmetic  4.85 us (4%)
  between operations  2.8 us (2%)
    pallas_call x1, Pallas kernels, exchange(): pl.pallas_call(tail_body, out_shape=(*(jax.ShapeDtypeStruct(h.shape, jnp....  53.7 us
    pallas_call x1, Pallas kernels, gather_halo(): pl.pallas_call(halo_body, out_shape=(*halo_shapes(tile), jax.ShapeDtypeSt...  33.6 us
    pallas_call x1, Pallas kernels, tile_gradient(): pl.pallas_call(body, out_shape=(jax.ShapeDtypeStruct(tile.shape, f32), *(...  17.6 us
    pallas_call x1, Pallas kernels, finish(): pl.pallas_call(finish_body, out_shape=(jax.ShapeDtypeStruct(tile.shape, f...  7.42 us

profile of v5, /device:TPU:1, one launch (start us, length us, event | category | flops | bytes accessed | tf_op | source)
XLA Modules:
  0.0 120.0 jit_solution(7061925973094666775)
XLA Ops:
  1.3 1.4 %fusion.5 = (s32[]{:T(128)}, pred[96,1]{0,1:T(4,128)(4,1)S(1)}, s32[96,1]{0,1:T(1,128)S(1)}) fusion(s32[]{:T(128)} %bitcast.41, s32[]{:T(128)S(6)} %mul.21, s32[96,2]{0,1:T(2,128)} %bitcast.47, s32[]{:T(128)S(6)} %mul.22), kind=kLoop, calls=%fused_computation.19 | loop fusion | flops 1247 | bytes 1264 | tf_op jit(solution)/shard_map/reduce_sum | solution.py:514
  4.0 0.6 pad_add_fusion.number_ref
  4.6 1.2 compare_convert_fusion.live_ref
  5.7 0.2 convert_reduce_fusion
  5.9 0.7 clamp_bitcast_fusion
  6.7 0.8 select_reduce_fusion.place_ref
  7.5 33.6 %gather_halo.1 = (f32[2,512,128]{2,1,0:T(8,128)}, f32[2,512,128]{2,1,0:T(8,128)}, f32[2,64,512]{2,1,0:T(8,128)}, f32[2,64,512]{2,1,0:T(8,128)}, f32[4,2,32,128]{...) custom-call(s32[8,96]{1,0:T(8,128)} %select_reduce_fusion.place_ref, ...), custom_call_target="tpu_custom_call" | custom-call | tf_op jit(solution)/shard_map/gather_halo/pallas_call | solution.py:470
  41.1 17.6 %tile_gradient.1 = (f32[2,1024,512]{2,1,0:T(8,128)}, f32[2,512,128]{2,1,0:T(8,128)}, f32[2,512,128]{2,1,0:T(8,128)}, f32[2,64,512]{2,1,0:T(8,128)}, f32[2,64,512...) custom-call(s32[8,96]{1,0:T(8,128)} %select_reduce_fusion.place_ref, s32[4]{0:T(128)} %pad_add_fusion.number_ref, ...), custom_call_target="tpu_custom_call" | custom-call | tf_op jit(solution)/shard_map/tile_gradient/pallas_call | solution.py:310
  58.8 53.7 %exchange.1 = (f32[2,512,128]{2,1,0:T(8,128)}, f32[2,512,128]{2,1,0:T(8,128)}, f32[2,64,512]{2,1,0:T(8,128)}, f32[2,64,512]{2,1,0:T(8,128)}, f32[4,2,32,128]{3,2...) custom-call(s32[8,96]{1,0:T(8,128)} %select_reduce_fusion.place_ref, f32[96]{0:T(128)} %compare_convert_fusion.live_ref, ...), custom_call_target="tpu_custom_call" | custom-call | tf_op jit(solution)/shard_map/exchange/pallas_call | solution.py:664
  112.4 7.4 %finish.1 = (f32[2,1024,512]{2,1,0:T(8,128)}, f32[16,32,128]{2,1,0:T(8,128)}) custom-call(s32[8,96]{1,0:T(8,128)} %select_reduce_fusion.place_ref, s32[4]{0:T(128)} %pad_add_fusion.number_ref, f32[2,1024,512]{2,1,0:T(8,128)} %get-tuple-element.32.tile_ref, f32[2,512,128]{2,1,0:T(8,128)} %get-tuple-element.39.left_ref, ...), custom_call_target="tpu_custom_call" | custom-call | tf_op jit(solution)/shard_map/finish/pallas_call | solution.py:775
  (8 shorter events, 0.1 us)

commit v6 on v5

--- a/solution.py
+++ b/solution.py
@@ -18,6 +18,7 @@
 SMALL = 4
 WIDE = 16
 STAGES = 7
+SLOTS = 96
 EARLY = 48
 LATE = 16
 
@@ -156,7 +157,7 @@
 
 
 def body(
-    place_ref, number_ref, probe_ref, w_ref, tile_ref, left_ref, right_ref, top_ref, bottom_ref, corner_ref,
+    place_ref, probe_ref, w_ref, tile_ref, left_ref, right_ref, top_ref, bottom_ref, corner_ref,
     measured_ref, patch_ref, part_ref,
     grad_tile, grad_left, grad_right, grad_top, grad_bottom, grad_corner, probe_out,
     obj, grad, held, sides, corners, patches, in_sems, held_sems, patch_sems,
@@ -164,8 +165,8 @@
     rows = tile_ref.shape[1]
     cols = tile_ref.shape[2]
     tiles = cols // WIN
-    begin, count, early = number_ref[0], number_ref[1], number_ref[2]
-    slots_max = place_ref.shape[1]
+    slots_max = measured_ref.shape[0]
+    begin, count, early = (place_ref[7, slots_max + i] for i in range(3))
 
     def fetch(place):
         turn = lax.rem(place - begin, AHEAD)
@@ -298,7 +299,7 @@
         copy.wait()
 
 
-def tile_gradient(places, numbers, probe, tile, halo, measured, patches, part):
+def tile_gradient(places, probe, tile, halo, measured, patches, part):
     planes, rows, cols = tile.shape
     tiles = cols // WIN
     f32 = jnp.float32
@@ -314,7 +315,7 @@
             *(jax.ShapeDtypeStruct(h.shape, f32) for h in halo),
             jax.ShapeDtypeStruct(probe.shape, f32),
         ),
-        in_specs=[smem, smem, vmem, vmem] + [hbm] * 8 + [vmem],
+        in_specs=[smem, vmem, vmem] + [hbm] * 8 + [vmem],
         out_specs=(*[hbm] * 6, vmem),
         scratch_shapes=[
             pltpu.VMEM(extent, f32),
@@ -329,7 +330,7 @@
         ],
         compiler_params=pltpu.CompilerParams(vmem_limit_bytes=56 * 1024 * 1024),
         name="tile_gradient",
-    )(places, numbers, probe, jnp.asarray(matrices()), tile, *halo, measured, patches, part)
+    )(places, probe, jnp.asarray(matrices()), tile, *halo, measured, patches, part)
 
 
 AROUND = ((-1, 0), (1, 0), (0, -1), (0, 1), (-1, -1), (-1, 1), (1, -1), (1, 1))
@@ -351,7 +352,7 @@
 
 
 def inner_patches(
-    begin, place_ref, live_ref, probe_ref, w_ref, obj, held, patches, patch_out, patch_sems, add
+    begin, place_ref, probe_ref, w_ref, obj, held, patches, patch_out, patch_sems, add
 ):
     size = patches.shape[1]
 
@@ -374,7 +375,7 @@
         def start(u):
             p = places[u]
             window = take(obj, place_ref[3, p], place_ref[4, p], place_ref[5, p], place_ref[6, p])
-            return slot_steps(window, probe_ref, held[place_ref[0, p]], live_ref[p], w_ref)
+            return slot_steps(window, probe_ref, held[place_ref[0, p]], place_ref[7, p].astype(jnp.float32), w_ref)
 
         def finish(u, grad_re, grad_im, terms):
             patches[turn, u, 0] = grad_re
@@ -390,9 +391,9 @@
 
 
 def halo_body(
-    place_ref, live_ref, probe_ref, w_ref, tile_ref, measured_ref,
-    left_out, right_out, top_out, bottom_out, corner_out, patch_out, part_out,
-    obj, held, packed, corners, patches, in_sems, held_sem, send_sems, recv_sems, patch_sems,
+    count_ref, position_ref, probe_ref, w_ref, tile_ref, measured_ref,
+    left_out, right_out, top_out, bottom_out, corner_out, patch_out, part_out, table_out,
+    table, place_ref, table_sems, obj, held, packed, corners, patches, in_sems, held_sem, send_sems, recv_sems, patch_sems,
 ):
     rows, cols = tile_ref.shape[1:]
     tiles = cols // WIN
@@ -425,6 +426,12 @@
         (corners.at[0], corner_out.at[3], (-1, -1)),
     )
     halo = send(moves, send_sems, recv_sems)
+    table[...] = ordered(position_ref[...], count_ref[0, 0], rows, cols)
+    keep = pltpu.make_async_copy(table, table_out, table_sems.at[0])
+    keep.start()
+    scalars = pltpu.make_async_copy(table, place_ref, table_sems.at[1])
+    scalars.start()
+    scalars.wait()
     for q in range(1, tiles - 1):
         loads[q].wait()
     measures.wait()
@@ -432,7 +439,8 @@
     def add(i, term):
         part_out[i // 2, i % 2] += term
 
-    inner_patches(0, place_ref, live_ref, probe_ref, w_ref, obj, held, patches, patch_out, patch_sems, add)
+    inner_patches(0, place_ref, probe_ref, w_ref, obj, held, patches, patch_out, patch_sems, add)
+    keep.wait()
     for copy in halo:
         copy.wait()
 
@@ -461,7 +469,7 @@
     return tuple(jax.ShapeDtypeStruct(s, jnp.float32) for s in shapes)
 
 
-def gather_halo(places, live, probe, tile, measured):
+def gather_halo(count, positions, probe, tile, measured):
     planes, rows, cols = tile.shape
     hbm = pl.BlockSpec(memory_space=pl.ANY)
     smem = pl.BlockSpec(memory_space=pltpu.SMEM)
@@ -473,10 +481,14 @@
             *halo_shapes(tile),
             jax.ShapeDtypeStruct((EARLY, planes, WIN, WIN), f32),
             jax.ShapeDtypeStruct(probe.shape, f32),
+            jax.ShapeDtypeStruct((8, WIN), jnp.int32),
         ),
-        in_specs=[smem, smem, vmem, vmem, hbm, hbm],
-        out_specs=(*[hbm] * 6, vmem),
+        in_specs=[smem, vmem, vmem, vmem, hbm, hbm],
+        out_specs=(*[hbm] * 6, vmem, hbm),
         scratch_shapes=[
+            pltpu.VMEM((8, WIN), jnp.int32),
+            pltpu.SMEM((8, WIN), jnp.int32),
+            pltpu.SemaphoreType.DMA((2,)),
             pltpu.VMEM((planes, cols // WIN, rows, WIN), f32),
             pltpu.VMEM(measured.shape, f32),
             pltpu.VMEM((2, planes, rows // 2, WIN), f32),
@@ -492,34 +504,41 @@
             collective_id=0, has_side_effects=True, vmem_limit_bytes=56 * 1024 * 1024
         ),
         name="gather_halo",
-    )(places, live, probe, jnp.asarray(matrices()), tile, measured)
+    )(count, positions, probe, jnp.asarray(matrices()), tile, measured)
 
 
 def ordered(positions, count, rows, cols):
     slots = positions.shape[0]
-    row = positions[:, 0] - lax.axis_index("ty") * rows
-    col = positions[:, 1] - lax.axis_index("tx") * cols
-    slot = jnp.arange(slots, dtype=jnp.int32)
+    row = positions[:, 0:1] - lax.axis_index("ty") * rows
+    col = positions[:, 1:2] - lax.axis_index("tx") * cols
+    shape = (slots, WIN)
+    slot = lax.broadcasted_iota(jnp.int32, (slots, 1), 0)
+    place = lax.broadcasted_iota(jnp.int32, shape, 1)
     inside = (row >= 0) & (row <= rows - WIN) & (col >= 0) & (col <= cols - WIN)
-    key = jnp.where(slot < count, jnp.where(inside, 0, 1), 2) * slots + slot
-    rank = jnp.sum((key[None, :] < key[:, None]).astype(jnp.int32), axis=1)
+    alive = slot < count
+    key = jnp.where(alive, jnp.where(inside, 0, 1), 2) * slots + slot
+    wide = jnp.broadcast_to(key, shape)
+    across = jnp.sum(jnp.where(place == slot, wide, 0), axis=0, keepdims=True)
+    across = jnp.where(lax.broadcasted_iota(jnp.int32, (1, WIN), 1) < slots, across, 4 * slots)
+    rank = jnp.sum(jnp.where(across < wide, 1, 0), axis=1, keepdims=True)
+    hit = jnp.broadcast_to(rank, shape) == place
     safe_row = jnp.clip(row, 0, rows - WIN)
     safe_col = jnp.clip(col, 0, cols - WIN)
     q = safe_col // WIN
-    table = jnp.stack(
-        [slot, row + RIM, col + WIN, safe_row, q, jnp.minimum(q + 1, cols // WIN - 1), safe_col % WIN, slot * 0]
-    )
-    hit = rank[None, :] == slot[:, None]
-    table = jnp.sum(jnp.where(hit[None], table[:, None, :], 0), axis=2)
-    inner = jnp.sum((inside & (slot < count)).astype(jnp.int32))
-    live = (slot < inner).astype(jnp.float32)
+    lines = (slot, row + RIM, col + WIN, safe_row, q, jnp.minimum(q + 1, cols // WIN - 1), safe_col - q * WIN)
+    lines = [jnp.sum(jnp.where(hit, line, 0), axis=0, keepdims=True) for line in lines]
+    inner = jnp.sum(jnp.where(inside & alive, 1, 0), axis=0, keepdims=True)
     early = jnp.minimum(inner, EARLY)
     done = jnp.minimum(inner, EARLY + LATE)
-    return table, live, jnp.stack([done, count, early, done - early])
+    at = lax.broadcasted_iota(jnp.int32, (1, WIN), 1)
+    last = jnp.where(at < inner, 1, 0)
+    for i, number in enumerate((done, count, early, done - early)):
+        last = jnp.where(at == slots + i, number, last)
+    return jnp.concatenate([*lines, last], axis=0)
 
 
 def tail_body(
-    place_ref, live_ref, probe_ref, w_ref, tile_ref, measured_ref,
+    place_ref, probe_ref, w_ref, tile_ref, measured_ref,
     left_ref, right_ref, top_ref, bottom_ref, corner_ref, start_ref,
     left_out, right_out, top_out, bottom_out, corner_out, patch_out, total_out,
     obj, held, patches, part_ref, gathered, stage, in_sems, held_sem, patch_sems,
@@ -599,7 +618,7 @@
         each = part_ref.shape[0] // 4
         part_ref[pl.ds(i * each, each)] += term.reshape(each, WIN // each, WIN)
 
-    inner_patches(EARLY, place_ref, live_ref, probe_ref, w_ref, obj, held, patches, patch_out, patch_sems, add)
+    inner_patches(EARLY, place_ref, probe_ref, w_ref, obj, held, patches, patch_out, patch_sems, add)
 
     @pl.loop(1, nx)
     def _(k):
@@ -654,7 +673,7 @@
         to_row(k).wait_send()
 
 
-def exchange(places, live, probe, tile, measured, halo, part):
+def exchange(places, probe, tile, measured, halo, part):
     hbm = pl.BlockSpec(memory_space=pl.ANY)
     vmem = pl.BlockSpec(memory_space=pltpu.VMEM)
     smem = pl.BlockSpec(memory_space=pltpu.SMEM)
@@ -668,7 +687,7 @@
             jax.ShapeDtypeStruct((LATE, planes, WIN, WIN), jnp.float32),
             jax.ShapeDtypeStruct((nx, *chunk), jnp.float32),
         ),
-        in_specs=[smem, smem, vmem, vmem] + [hbm] * 7 + [vmem],
+        in_specs=[smem, vmem, vmem] + [hbm] * 7 + [vmem],
         out_specs=(*[hbm] * 6, vmem),
         scratch_shapes=[
             pltpu.VMEM((planes, cols // WIN, rows, WIN), jnp.float32),
@@ -693,18 +712,18 @@
             collective_id=1, has_side_effects=True, vmem_limit_bytes=56 * 1024 * 1024
         ),
         name="exchange",
-    )(places, live, probe, jnp.asarray(matrices()), tile, measured, *halo, part.reshape(nx, *chunk))
+    )(places, probe, jnp.asarray(matrices()), tile, measured, *halo, part.reshape(nx, *chunk))
 
 
 def finish_body(
-    place_ref, number_ref, tile_ref, left_ref, right_ref, top_ref, bottom_ref, corner_ref, patch_ref, total_ref,
+    place_ref, tile_ref, left_ref, right_ref, top_ref, bottom_ref, corner_ref, patch_ref, total_ref,
     out_ref, total_out, grad, sides, rims, corners, patches, in_sems, more_sems,
 ):
     planes, rows, cols = tile_ref.shape
     tiles = cols // WIN
     ty, tx = lax.axis_index("ty"), lax.axis_index("tx")
     ny, nx = lax.axis_size("ty"), lax.axis_size("tx")
-    late = number_ref[3]
+    late = place_ref[7, SLOTS + 3]
     spans = [pl.ds(q * WIN, WIN) for q in range(tiles)]
     more = (
         (patch_ref, patches),
@@ -716,26 +735,18 @@
     )
     more = [pltpu.make_async_copy(a, b, more_sems.at[i]) for i, (a, b) in enumerate(more)]
     reads = [
-        pltpu.make_async_copy(tile_ref.at[:, :, span], grad.at[:, q], in_sems.at[q]) for q, span in enumerate(spans)
+        [
+            pltpu.make_async_copy(tile_ref.at[p, :, span], grad.at[p, q], in_sems.at[p, q])
+            for q, span in enumerate(spans)
+        ]
+        for p in range(planes)
     ]
-    for copy in reads + more:
+    for copy in (more[0], *reads[0], *more[1:], *reads[1]):
         copy.start()
     total_out[...] = total_ref[...]
     no_side = (tx == 0, tx == nx - 1)
     no_end = (ty == 0, ty == ny - 1)
     ends = (0, rows - RIM)
-    for copy in (*reads, more[0]):
-        copy.wait()
-
-    def info_of(place):
-        at = EARLY + place
-        return place_ref[3, at], place_ref[4, at], place_ref[6, at], place_ref[5, at]
-
-    for first in range(0, patches.shape[0], U):
-        deposit(grad, patches, info_of, first, late)
-
-    for copy in more[1:]:
-        copy.wait()
 
     def side_add(plane, side, start, packed, gone):
         high = side == 1
@@ -747,7 +758,24 @@
             value = jnp.where(gone, 0.0, value)
             grad[plane, side * (tiles - 1), here, :] += jnp.where(mine, value, 0.0)
 
-    for plane in range(2):
+    for plane in range(planes):
+        for copy in reads[plane]:
+            copy.wait()
+        if plane == 0:
+            more[0].wait()
+        for place in range(patches.shape[0]):
+            @pl.when(place < late)
+            def _(place=place):
+                at = EARLY + place
+                row, q, q_next, shift = place_ref[3, at], place_ref[4, at], place_ref[5, at], place_ref[6, at]
+                here = pl.ds(row, WIN)
+                after = lax.broadcasted_iota(jnp.int32, (WIN, WIN), 1) >= shift
+                turned = pltpu.roll(patches[place, plane], shift, 1)
+                grad[plane, q, here, :] += jnp.where(after, turned, 0.0)
+                grad[plane, q_next, here, :] += jnp.where(after, 0.0, turned)
+        if plane == 0:
+            for copy in more[1:]:
+                copy.wait()
         for side in range(2):
             side_add(plane, side, 0, sides[side, plane], no_side[side])
             for end in range(2):
@@ -757,16 +785,14 @@
             for q in range(tiles):
                 value = jnp.where(no_end[end], 0.0, rims[end, plane, :, spans[q]])
                 grad[plane, q, pl.ds(ends[end], RIM), :] += value
-    writes = [
-        pltpu.make_async_copy(grad.at[:, q], out_ref.at[:, :, span], in_sems.at[q]) for q, span in enumerate(spans)
-    ]
-    for copy in writes:
-        copy.start()
-    for copy in writes:
-        copy.wait()
-
-
-def finish(places, numbers, tile, halo, patches, total):
+        for q in range(tiles):
+            pltpu.make_async_copy(grad.at[plane, q], out_ref.at[plane, :, spans[q]], in_sems.at[plane, q]).start()
+    for plane in range(planes):
+        for q in range(tiles):
+            pltpu.make_async_copy(grad.at[plane, q], out_ref.at[plane, :, spans[q]], in_sems.at[plane, q]).wait()
+
+
+def finish(places, tile, halo, patches, total):
     planes, rows, cols = tile.shape
     hbm = pl.BlockSpec(memory_space=pl.ANY)
     vmem = pl.BlockSpec(memory_space=pltpu.VMEM)
@@ -775,7 +801,7 @@
     return pl.pallas_call(
         finish_body,
         out_shape=(jax.ShapeDtypeStruct(tile.shape, f32), jax.ShapeDtypeStruct(total.shape, f32)),
-        in_specs=[smem, smem] + [hbm] * 7 + [vmem],
+        in_specs=[smem] + [hbm] * 7 + [vmem],
         out_specs=(hbm, vmem),
         scratch_shapes=[
             pltpu.VMEM((planes, cols // WIN, rows, WIN), f32),
@@ -783,22 +809,21 @@
             pltpu.VMEM((2, planes, RIM, cols), f32),
             pltpu.VMEM((4, planes, RIM // 2, WIN), f32),
             pltpu.VMEM(patches.shape, f32),
-            pltpu.SemaphoreType.DMA((cols // WIN,)),
+            pltpu.SemaphoreType.DMA((planes, cols // WIN)),
             pltpu.SemaphoreType.DMA((6,)),
         ],
         compiler_params=pltpu.CompilerParams(vmem_limit_bytes=56 * 1024 * 1024),
         name="finish",
-    )(places, numbers, tile, *halo, patches, total)
+    )(places, tile, *halo, patches, total)
 
 
 def shards(object_planes, probe, positions, counts, amplitudes):
     planes, rows, cols = object_planes.shape
-    places, live, numbers = ordered(positions[0, 0], counts[0, 0], rows, cols)
     measured = amplitudes[0, 0]
-    *halo, patches, early_part = gather_halo(places, live, probe, object_planes, measured)
-    tile, *outer, part = tile_gradient(places, numbers, probe, object_planes, halo, measured, patches, early_part)
-    *outer, patches, total = exchange(places, live, probe, object_planes, measured, outer, part)
-    tile, total = finish(places, numbers, tile, outer, patches, total)
+    *halo, patches, early_part, places = gather_halo(counts, positions[0, 0], probe, object_planes, measured)
+    tile, *outer, part = tile_gradient(places, probe, object_planes, halo, measured, patches, early_part)
+    *outer, patches, total = exchange(places, probe, object_planes, measured, outer, part)
+    tile, total = finish(places, tile, outer, patches, total)
     return tile, total.reshape(probe.shape)
 
 

time: 120 us -> 118 us (0.983)
  other arithmetic: 4.85 us -> 0 us
  Pallas kernels: 112 us -> 114 us
  local copies, waits for them, and re-layouts: 0.03 us -> 1.4 us
  between operations: 2.8 us -> 1.46 us
    pallas_call x1, Pallas kernels: 53.7 us -> 56.7 us  [exchange(): pl.pallas_call(tail_body, out_shape=(*(jax.ShapeDtypeStruct(h.shape, jnp....]
    reduce_sum x3 -> x0, other arithmetic: 2.38 us -> none  [the longest x1 1.4 us: ordered(): inner = jnp.sum((inside & (slot < count)).astype(jnp.int32))]
    unnamed x0 -> x1, local copies, waits for them, and re-layouts: none -> 1.4 us
where the time goes in v6:
time: 118 us; the launch traced here: 117 us
  Pallas kernels  114 us (97%)
  between operations  1.46 us (1%)
  local copies, waits for them, and re-layouts  1.4 us (1%)
    pallas_call x1, Pallas kernels, exchange(): pl.pallas_call(tail_body, out_shape=(*(jax.ShapeDtypeStruct(h.shape, jnp....  56.7 us
    pallas_call x1, Pallas kernels, gather_halo(): pl.pallas_call(halo_body, out_shape=(*halo_shapes(tile), jax.ShapeDtypeSt...  33.6 us
    pallas_call x1, Pallas kernels, tile_gradient(): pl.pallas_call(body, out_shape=(jax.ShapeDtypeStruct(tile.shape, f32), *(...  16.9 us
    pallas_call x1, Pallas kernels, finish(): pl.pallas_call(finish_body, out_shape=(jax.ShapeDtypeStruct(tile.shape, f...  7.14 us

profile of v6, /device:TPU:1, one launch (start us, length us, event | category | flops | bytes accessed | tf_op | source)
XLA Modules:
  0.0 117.2 jit_solution(4206134366784655802)
XLA Ops:
  1.3 1.4 %copy.10 = s32[1,1,96,2]{3,2,1,0:T(8,128)} copy(s32[1,1,96,2]{2,3,1,0:T(2,128)} %param.10) | data formatting | bytes 1536 | tf_op args[2]
  2.7 33.6 %gather_halo.1 = (f32[2,512,128]{2,1,0:T(8,128)}, f32[2,512,128]{2,1,0:T(8,128)}, f32[2,64,512]{2,1,0:T(8,128)}, f32[2,64,512]{2,1,0:T(8,128)}, f32[4,2,32,128]{...) custom-call(s32[1,1]{1,0:T(1,128)S(6)} %copy.11.count_ref, ...), custom_call_target="tpu_custom_call" | custom-call | tf_op jit(solution)/shard_map/gather_halo/pallas_call | solution.py:478
  36.3 16.9 %tile_gradient.1 = (f32[2,1024,512]{2,1,0:T(8,128)}, f32[2,512,128]{2,1,0:T(8,128)}, f32[2,512,128]{2,1,0:T(8,128)}, f32[2,64,512]{2,1,0:T(8,128)}, f32[2,64,512...) custom-call(s32[8,128]{1,0:T(8,128)} %get-tuple-element.26.place_ref, ...), custom_call_target="tpu_custom_call" | custom-call | tf_op jit(solution)/shard_map/tile_gradient/pallas_call | solution.py:311
  53.2 56.7 %exchange.1 = (f32[2,512,128]{2,1,0:T(8,128)}, f32[2,512,128]{2,1,0:T(8,128)}, f32[2,64,512]{2,1,0:T(8,128)}, f32[2,64,512]{2,1,0:T(8,128)}, f32[4,2,32,128]{3,2...) custom-call(s32[8,128]{1,0:T(8,128)} %get-tuple-element.26.place_ref, f32[2,2,128,128]{3,2,1,0:T(8,128)} %probe_ref.5, ...), custom_call_target="tpu_custom_call" | custom-call | tf_op jit(solution)/shard_map/exchange/pallas_call | solution.py:683
  109.9 7.1 %finish.1 = (f32[2,1024,512]{2,1,0:T(8,128)}, f32[16,32,128]{2,1,0:T(8,128)}) custom-call(s32[8,128]{1,0:T(8,128)} %get-tuple-element.26.place_ref, f32[2,1024,512]{2,1,0:T(8,128)} %get-tuple-element.34.tile_ref, f32[2,512,128]{2,1,0:T(8,128)} %get-tuple-element.41.left_ref, f32[2,512,128]{2,1,0:T(8,128)} %get-tuple-element.42.right_ref, ...), custom_call_target="tpu_custom_call" | custom-call | tf_op jit(solution)/shard_map/finish/pallas_call | solution.py:801

commit v7 on v6

--- a/solution.py
+++ b/solution.py
@@ -18,7 +18,6 @@
 SMALL = 4
 WIDE = 16
 STAGES = 7
-SLOTS = 96
 EARLY = 48
 LATE = 16
 
@@ -148,12 +147,10 @@
     return (turned, packed) if high else (packed, turned)
 
 
-def deposit(grad, patches, info_of, first, end):
-    for u in range(U):
-        @pl.when(first + u < end)
-        def _(place=first + u):
-            row, q, shift, q_next = info_of(place)
-            put(grad, row, q, shift, (patches[place, 0], patches[place, 1]), q_next)
+def deposit(grad, patches, info_of, first):
+    for place in range(first, first + U):
+        row, q, shift, q_next = info_of(place)
+        put(grad, row, q, shift, (patches[place, 0], patches[place, 1]), q_next)
 
 
 def body(
@@ -166,7 +163,7 @@
     cols = tile_ref.shape[2]
     tiles = cols // WIN
     slots_max = measured_ref.shape[0]
-    begin, count, early = (place_ref[7, slots_max + i] for i in range(3))
+    begin, count = (place_ref[7, slots_max + i] for i in range(2))
 
     def fetch(place):
         turn = lax.rem(place - begin, AHEAD)
@@ -207,7 +204,7 @@
 
     for i, copy in enumerate(chunks):
         copy.wait()
-        deposit(grad, patches, info_of, i * U, early)
+        deposit(grad, patches, info_of, i * U)
     for copy in loads:
         copy.wait()
     for plane in range(2):
@@ -408,12 +405,6 @@
     measures.start()
     part_out[...] = jnp.zeros_like(part_out)
     above, below = pl.ds(0, RIM), pl.ds(rows - RIM, RIM)
-    for side, q in enumerate((0, tiles - 1)):
-        loads[q].wait()
-        for plane in range(2):
-            packed[side, plane] = pack(obj[plane, q], side == 1)
-            corners[side, plane] = pack(obj[plane, q, above, :], side == 1)
-            corners[2 + side, plane] = pack(obj[plane, q, below, :], side == 1)
     pl.semaphore_wait(pltpu.get_barrier_semaphore(), len(AROUND))
     moves = (
         (packed.at[0], right_out, (0, -1)),
@@ -425,7 +416,17 @@
         (corners.at[1], corner_out.at[2], (-1, 1)),
         (corners.at[0], corner_out.at[3], (-1, -1)),
     )
-    halo = send(moves, send_sems, recv_sems)
+    halo = send(moves, send_sems, recv_sems, begin=False)
+    for copy in halo[2:4]:
+        copy.start()
+    for side, q in enumerate((0, tiles - 1)):
+        loads[q].wait()
+        for plane in range(2):
+            packed[side, plane] = pack(obj[plane, q], side == 1)
+            corners[side, plane] = pack(obj[plane, q, above, :], side == 1)
+            corners[2 + side, plane] = pack(obj[plane, q, below, :], side == 1)
+    for copy in (*halo[:2], *halo[4:]):
+        copy.start()
     table[...] = ordered(position_ref[...], count_ref[0, 0], rows, cols)
     keep = pltpu.make_async_copy(table, table_out, table_sems.at[0])
     keep.start()
@@ -508,9 +509,15 @@
 
 
 def ordered(positions, count, rows, cols):
-    slots = positions.shape[0]
-    row = positions[:, 0:1] - lax.axis_index("ty") * rows
-    col = positions[:, 1:2] - lax.axis_index("tx") * cols
+    slots = positions.shape[1]
+    square = (slots, slots)
+    same = lax.broadcasted_iota(jnp.int32, square, 0) == lax.broadcasted_iota(jnp.int32, square, 1)
+
+    def upright(line):
+        return jnp.sum(jnp.where(same, jnp.broadcast_to(line, square), 0), axis=1, keepdims=True)
+
+    row = upright(positions[0:1]) - lax.axis_index("ty") * rows
+    col = upright(positions[1:2]) - lax.axis_index("tx") * cols
     shape = (slots, WIN)
     slot = lax.broadcasted_iota(jnp.int32, (slots, 1), 0)
     place = lax.broadcasted_iota(jnp.int32, shape, 1)
@@ -723,7 +730,6 @@
     tiles = cols // WIN
     ty, tx = lax.axis_index("ty"), lax.axis_index("tx")
     ny, nx = lax.axis_size("ty"), lax.axis_size("tx")
-    late = place_ref[7, SLOTS + 3]
     spans = [pl.ds(q * WIN, WIN) for q in range(tiles)]
     more = (
         (patch_ref, patches),
@@ -764,15 +770,13 @@
         if plane == 0:
             more[0].wait()
         for place in range(patches.shape[0]):
-            @pl.when(place < late)
-            def _(place=place):
-                at = EARLY + place
-                row, q, q_next, shift = place_ref[3, at], place_ref[4, at], place_ref[5, at], place_ref[6, at]
-                here = pl.ds(row, WIN)
-                after = lax.broadcasted_iota(jnp.int32, (WIN, WIN), 1) >= shift
-                turned = pltpu.roll(patches[place, plane], shift, 1)
-                grad[plane, q, here, :] += jnp.where(after, turned, 0.0)
-                grad[plane, q_next, here, :] += jnp.where(after, 0.0, turned)
+            at = EARLY + place
+            row, q, q_next, shift = place_ref[3, at], place_ref[4, at], place_ref[5, at], place_ref[6, at]
+            here = pl.ds(row, WIN)
+            after = lax.broadcasted_iota(jnp.int32, (WIN, WIN), 1) >= shift
+            turned = pltpu.roll(patches[place, plane], shift, 1)
+            grad[plane, q, here, :] += jnp.where(after, turned, 0.0)
+            grad[plane, q_next, here, :] += jnp.where(after, 0.0, turned)
         if plane == 0:
             for copy in more[1:]:
                 copy.wait()
@@ -820,7 +824,7 @@
 def shards(object_planes, probe, positions, counts, amplitudes):
     planes, rows, cols = object_planes.shape
     measured = amplitudes[0, 0]
-    *halo, patches, early_part, places = gather_halo(counts, positions[0, 0], probe, object_planes, measured)
+    *halo, patches, early_part, places = gather_halo(counts, positions[0, 0].T, probe, object_planes, measured)
     tile, *outer, part = tile_gradient(places, probe, object_planes, halo, measured, patches, early_part)
     *outer, patches, total = exchange(places, probe, object_planes, measured, outer, part)
     tile, total = finish(places, tile, outer, patches, total)

time: 118 us -> 115 us (0.975)
  local copies, waits for them, and re-layouts: 1.4 us -> 0 us
    pallas_call x1, Pallas kernels: 16.9 us -> 14.8 us  [tile_gradient(): pl.pallas_call(body, out_shape=(jax.ShapeDtypeStruct(tile.shape, f32), *(...]
    unnamed x1 -> x0, local copies, waits for them, and re-layouts: 1.4 us -> none
where the time goes in v7:
time: 115 us
  Pallas kernels  113 us (98%)
  between operations  1.48 us (1%)
    pallas_call x1, Pallas kernels, exchange(): pl.pallas_call(tail_body, out_shape=(*(jax.ShapeDtypeStruct(h.shape, jnp....  56.8 us
    pallas_call x1, Pallas kernels, gather_halo(): pl.pallas_call(halo_body, out_shape=(*halo_shapes(tile), jax.ShapeDtypeSt...  34.6 us
    pallas_call x1, Pallas kernels, tile_gradient(): pl.pallas_call(body, out_shape=(jax.ShapeDtypeStruct(tile.shape, f32), *(...  14.8 us
    pallas_call x1, Pallas kernels, finish(): pl.pallas_call(finish_body, out_shape=(jax.ShapeDtypeStruct(tile.shape, f...  7.14 us

profile of v7, /device:TPU:1, one launch (start us, length us, event | category | flops | bytes accessed | tf_op | source)
XLA Modules:
  0.0 114.8 jit_solution(6867976416741920603)
XLA Ops:
  1.3 34.6 %gather_halo.1 = (f32[2,512,128]{2,1,0:T(8,128)}, f32[2,512,128]{2,1,0:T(8,128)}, f32[2,64,512]{2,1,0:T(8,128)}, f32[2,64,512]{2,1,0:T(8,128)}, f32[4,2,32,128]{...) custom-call(s32[1,1]{1,0:T(1,128)S(6)} %copy.10.count_ref, ...), custom_call_target="tpu_custom_call" | custom-call | tf_op jit(solution)/shard_map/gather_halo/pallas_call | solution.py:479
  35.9 14.8 %tile_gradient.1 = (f32[2,1024,512]{2,1,0:T(8,128)}, f32[2,512,128]{2,1,0:T(8,128)}, f32[2,512,128]{2,1,0:T(8,128)}, f32[2,64,512]{2,1,0:T(8,128)}, f32[2,64,512...) custom-call(s32[8,128]{1,0:T(8,128)} %get-tuple-element.26.place_ref, ...), custom_call_target="tpu_custom_call" | custom-call | tf_op jit(solution)/shard_map/tile_gradient/pallas_call | solution.py:308
  50.7 56.8 %exchange.1 = (f32[2,512,128]{2,1,0:T(8,128)}, f32[2,512,128]{2,1,0:T(8,128)}, f32[2,64,512]{2,1,0:T(8,128)}, f32[2,64,512]{2,1,0:T(8,128)}, f32[4,2,32,128]{3,2...) custom-call(s32[8,128]{1,0:T(8,128)} %get-tuple-element.26.place_ref, f32[2,2,128,128]{3,2,1,0:T(8,128)} %probe_ref.5, ...), custom_call_target="tpu_custom_call" | custom-call | tf_op jit(solution)/shard_map/exchange/pallas_call | solution.py:690
  107.5 7.1 %finish.1 = (f32[2,1024,512]{2,1,0:T(8,128)}, f32[16,32,128]{2,1,0:T(8,128)}) custom-call(s32[8,128]{1,0:T(8,128)} %get-tuple-element.26.place_ref, f32[2,1024,512]{2,1,0:T(8,128)} %get-tuple-element.34.tile_ref, f32[2,512,128]{2,1,0:T(8,128)} %get-tuple-element.41.left_ref, f32[2,512,128]{2,1,0:T(8,128)} %get-tuple-element.42.right_ref, ...), custom_call_target="tpu_custom_call" | custom-call | tf_op jit(solution)/shard_map/finish/pallas_call | solution.py:805
